TPU v7x, 256 devices: a whole 4x4x8 slice. The times are simulated.
256 devices in a mesh: pool: 64 (over y, z, core), tp: 4 (over x).
Axes of the slice: x: 4, y: 4, z: 8, core: 2. Of those that a mesh axis runs over, the one named last changes fastest.
Arguments:
- normed_input: bfloat16 [2, 3072, 8192], P(None, 'pool', 'tp'), may hold values from -6 to 6
- base_query_output: bfloat16 [2, 3072, 8192], P(None, 'pool', 'tp'), may hold values from -4.5 to 4.5
- adapter_down_weight: bfloat16 [8192, 512, 64], P('tp', 'pool'), may hold values from -0.0625 to 0.0625
- adapter_up_weight: bfloat16 [512, 64, 8192], P('pool', None, 'tp'), may hold values from -0.75 to 0.75
- row_adapter_index: int32 [3072], P('pool'), may hold values from 0 to 511, as said below
- paged_key_cache: bfloat16 [12288, 32, 8, 128], P('pool', None, 'tp'), may hold values from -4.5 to 4.5
- paged_value_cache: bfloat16 [12288, 32, 8, 128], P('pool', None, 'tp'), may hold values from -6 to 6
- step_token_keys: bfloat16 [2, 3072, 8, 128], P(None, 'pool', 'tp'), may hold values from -6 to 6
- step_token_values: bfloat16 [2, 3072, 8, 128], P(None, 'pool', 'tp'), may hold values from -6 to 6
- row_page_table: int32 [3072, 4], P('pool'), may hold values from 0 to 191, as said below
- lengths: int32 [3072], P('pool'), may hold values from 1 to 128, as said below
Outputs:
- attended: bfloat16 [2, 3072, 8192], P(None, 'pool', 'tp')
Inputs may be any that keep to these rules, and one draw needn't show every extreme that they name: Adapter ids name the pool index row_adapter_index // 8; among the rows of one device at most 2 name adapters of one pool index, and in every device some 2 rows do. `row_page_table`: each device's rows of the table hold each of its 192 pages exactly once. `lengths`: every device has a row with 128 cached tokens.
All inputs are finite; a program needn't handle non-finite values.
Results may differ from a plain program's by a relative error of at most 0.0059.
Values may be sent and summed in bfloat16 or wider, within the bound.
A program may use at most 64 MiB of HBM per device.

v0:
```python
import jax
import jax.numpy as jnp
from jax import lax
from jax.sharding import PartitionSpec as P

ADAPTER_SCALE = 0.5


def project_down(received, got_ids, joined_down_weight, adapter_weights, adapter_rank_size):
    lead = received.shape[:-1]
    proj = jnp.dot(received, joined_down_weight, preferred_element_type=jnp.float32)
    proj = proj.reshape(lead + (adapter_weights, adapter_rank_size))
    pick = (got_ids[..., None] == jnp.arange(adapter_weights, dtype=jnp.int32)).astype(jnp.float32)
    return (jnp.sum(proj * pick[..., None], axis=-2), pick)


def project_up(u_bf, pick, joined_up_weight):
    lead = u_bf.shape[:-1]
    expanded_rows = (pick[..., None].astype(jnp.bfloat16) * u_bf[..., None, :]).reshape(
        -1, joined_up_weight.shape[0]
    )
    query_correction = (
        jnp.dot(expanded_rows, joined_up_weight, preferred_element_type=jnp.float32) * ADAPTER_SCALE
    )
    return query_correction.astype(jnp.bfloat16)


def adapter_step_update(
    input_rows,
    place_halfwidth,
    slot_index_list,
    joined_down_weight,
    joined_up_weight,
    adapter_weights,
    adapter_rank_size,
):
    x_slots = jnp.dot(place_halfwidth, input_rows, preferred_element_type=jnp.float32).astype(
        jnp.bfloat16
    )
    received, got_ids = (
        lax.all_to_all(x_slots, "pool", split_axis=0, concat_axis=0, tiled=True),
        lax.all_to_all(slot_index_list, "pool", split_axis=0, concat_axis=0, tiled=True),
    )
    u_part, pick = project_down(
        received, got_ids, joined_down_weight, adapter_weights, adapter_rank_size
    )
    u_bf = lax.psum(u_part, "tp").astype(jnp.bfloat16)
    query_correction = project_up(u_bf, pick, joined_up_weight)
    returned = lax.all_to_all(query_correction, "pool", split_axis=0, concat_axis=0, tiled=True)
    return jnp.dot(place_halfwidth.T, returned, preferred_element_type=jnp.float32)


def attend_all(query, keys, values, extra_keys, extra_values, lengths):
    rows, ctx, kvn, head = keys.shape
    inv = 1.0 / jnp.sqrt(jnp.float32(head))
    grouped = query.reshape(rows, kvn, -1, head)
    s_old = jnp.einsum("rkgh,rtkh->rkgt", grouped, keys, preferred_element_type=jnp.float32) * inv
    live = jnp.arange(ctx, dtype=jnp.int32)[None, :] < lengths[:, None]
    s_old = jnp.where(live[:, None, None, :], s_old, jnp.float32(-1e30))
    s_new = (
        jnp.einsum("rkgh,rekh->rkge", grouped, extra_keys, preferred_element_type=jnp.float32) * inv
    )
    top = jnp.maximum(jnp.max(s_old, axis=-1), jnp.max(s_new, axis=-1))[..., None]
    e_old = jnp.exp(s_old - top)
    e_new = jnp.exp(s_new - top)
    total = jnp.sum(e_old, axis=-1, keepdims=True) + jnp.sum(e_new, axis=-1, keepdims=True)
    p_old = (e_old / total).astype(jnp.bfloat16)
    p_new = (e_new / total).astype(jnp.bfloat16)
    out = jnp.einsum("rkgt,rtkh->rkgh", p_old, values, preferred_element_type=jnp.float32)
    out = out + jnp.einsum(
        "rkge,rekh->rkgh", p_new, extra_values, preferred_element_type=jnp.float32
    )
    return out.reshape(rows, -1).astype(jnp.bfloat16)


def shards(
    normed_input,
    base_query_output,
    adapter_down_weight,
    adapter_up_weight,
    row_adapter_index,
    paged_key_cache,
    paged_value_cache,
    step_token_keys,
    step_token_values,
    row_page_table,
    lengths,
):
    rows = row_adapter_index.shape[0]
    adapter_weights = adapter_up_weight.shape[0]
    adapter_rank_size = adapter_up_weight.shape[1]
    owners = lax.axis_size("pool")
    capacity = 2 + (rows - 2) // owners
    joined_down_weight = adapter_down_weight.reshape(
        adapter_down_weight.shape[0], adapter_weights * adapter_rank_size
    )
    joined_up_weight = adapter_up_weight.reshape(
        adapter_weights * adapter_rank_size, adapter_up_weight.shape[2]
    )
    owner = row_adapter_index // adapter_weights
    local = row_adapter_index % adapter_weights
    order = jnp.arange(rows, dtype=jnp.int32)
    earlier = jnp.sum(
        ((owner[None, :] == owner[:, None]) & (order[None, :] < order[:, None])).astype(jnp.int32),
        axis=1,
    )
    slot = owner * capacity + earlier
    place = jnp.arange(owners * capacity, dtype=jnp.int32)[:, None] == slot[None, :]
    place_halfwidth = place.astype(jnp.bfloat16)
    slot_index_list = jnp.sum(jnp.where(place, local[None, :], 0), axis=1)
    deltas = [
        adapter_step_update(
            normed_input[decode_step],
            place_halfwidth,
            slot_index_list,
            joined_down_weight,
            joined_up_weight,
            adapter_weights,
            adapter_rank_size,
        )
        for decode_step in range(2)
    ]
    kvn = paged_key_cache.shape[2]
    head = paged_key_cache.shape[3]
    keys = paged_key_cache[row_page_table].reshape(rows, -1, kvn, head)
    values = paged_value_cache[row_page_table].reshape(rows, -1, kvn, head)
    results = []
    for decode_step in range(2):
        query = (base_query_output[decode_step].astype(jnp.float32) + deltas[decode_step]).astype(
            jnp.bfloat16
        )
        extra_keys = jnp.moveaxis(step_token_keys[: decode_step + 1], 0, 1)
        extra_values = jnp.moveaxis(step_token_values[: decode_step + 1], 0, 1)
        results.append(attend_all(query, keys, values, extra_keys, extra_values, lengths))
    return jnp.stack(results, axis=0)


def solution(mesh):
    placed = (
        P(None, "pool", "tp"),
        P(None, "pool", "tp"),
        P("tp", "pool", None),
        P("pool", None, "tp"),
        P("pool"),
        P("pool", None, "tp", None),
        P("pool", None, "tp", None),
        P(None, "pool", "tp", None),
        P(None, "pool", "tp", None),
        P("pool", None),
        P("pool"),
    )
    return jax.shard_map(
        shards, mesh=mesh, in_specs=placed, out_specs=P(None, "pool", "tp"), check_vma=False
    )
```

profile of v0, /device:TPU:1, one launch (start us, length us, event | category | flops | bytes accessed | tf_op | source)
XLA Modules:
  0.0 186.3 jit_solution(6986713209031900041)
XLA Ops:
  1.9 13.2 %all-to-all-start = ((s32[64,2,1]{1,2,0:T(1,128)}), s32[64,2,1]{1,2,0:T(1,128)S(1)}, u32[]{:S(2)}, u32[]{:S(2)}) async-start(s32[64,2,1]{1,2,0:T(1,128)} %bitcast.1), calls=%async_computation | async-start | bytes 65536 | tf_op jit(solution)/shard_map/all_to_all | solution.py:42
  15.1 2.1 %convolution_convert_fusion = bf16[128,2048]{1,0:T(8,128)(2,1)} fusion(bf16[2,48,2048]{2,1,0:T(8,128)(2,1)} %param.11, s32[48]{0:T(128)S(1)} %multiply_add_fusion), kind=kOutput, calls=%fused_computation.16 | convolution fusion | flops 25434112 | bytes 721088 | tf_op jit(solution)/shard_map/dot_general | solution.py:37
  17.2 2.2 %all_to_all.47 = bf16[64,2,2048]{2,1,0:T(2,128)(2,1)} reshape(bf16[128,2048]{1,0:T(8,128)(2,1)} %convolution_convert_fusion) | data formatting | bytes 1048576 | tf_op jit(solution)/shard_map/all_to_all | solution.py:41
  19.4 4.9 %all-to-all-done = s32[64,2,1]{1,2,0:T(1,128)S(1)} async-done(((s32[64,2,1]{1,2,0:T(1,128)}), s32[64,2,1]{1,2,0:T(1,128)S(1)}, u32[]{:S(2)}, u32[]{:S(2)}) %all-to-all-start) | async-done | bytes 544 | tf_op jit(solution)/shard_map/all_to_all | solution.py:42
  24.3 5.6 %all-to-all-start.3 = ((bf16[64,2,2048]{2,1,0:T(2,128)(2,1)}), bf16[64,2,2048]{2,1,0:T(2,128)(2,1)}, u32[]{:S(2)}, u32[]{:S(2)}) async-start(bf16[64,2,2048]{2,1,0:T(2,128)(2,1)} %all_to_all.47), calls=%async_computation.3 | async-start | bytes 1048576 | tf_op jit(solution)/shard_map/all_to_all | solution.py:41
  29.9 2.2 %convolution_convert_fusion.1 = bf16[128,2048]{1,0:T(8,128)(2,1)} fusion(bf16[2,48,2048]{2,1,0:T(8,128)(2,1)} %param.11, s32[48]{0:T(128)S(1)} %multiply_add_fusion), kind=kOutput, calls=%fused_computation.17 | convolution fusion | flops 25434112 | bytes 721088 | tf_op jit(solution)/shard_map/dot_general | solution.py:37
  32.1 2.2 %all_to_all.41 = bf16[64,2,2048]{2,1,0:T(2,128)(2,1)} reshape(bf16[128,2048]{1,0:T(8,128)(2,1)} %convolution_convert_fusion.1) | data formatting | bytes 1048576 | tf_op jit(solution)/shard_map/all_to_all | solution.py:41
  34.2 12.9 %all-to-all-done.3 = bf16[64,2,2048]{2,1,0:T(2,128)(2,1)} async-done(((bf16[64,2,2048]{2,1,0:T(2,128)(2,1)}), bf16[64,2,2048]{2,1,0:T(2,128)(2,1)}, u32[]{:S(2)}, u32[]{:S(2)}) %all-to-all-start.3) | async-done | bytes 524320 | tf_op jit(solution)/shard_map/all_to_all | solution.py:41
  47.1 6.5 %all-to-all-start.1 = ((bf16[64,2,2048]{2,1,0:T(2,128)(2,1)}), bf16[64,2,2048]{2,1,0:T(2,128)(2,1)}, u32[]{:S(2)}, u32[]{:S(2)}) async-start(bf16[64,2,2048]{2,1,0:T(2,128)(2,1)} %all_to_all.41), calls=%async_computation.1 | async-start | bytes 1048576 | tf_op jit(solution)/shard_map/all_to_all | solution.py:41
  57.3 2.5 %fusion.45 = f32[128,64]{0,1:T(8,128)S(1)} fusion(bf16[128,2048,1]{1,0,2:T(8,128)(2,1)} %reshape.210, bf16[2048,8,64]{0,2,1:T(8,128)(2,1)} %param.13, f32[128,8]{0,1:T(8,128)S(1)} %get-tuple-element.10), kind=kOutput, calls=%fused_computation.38 | convolution fusion | flops 268558336 | bytes 2658304 | tf_op jit(solution)/shard_map/dot_general | solution.py:11
  59.8 11.1 %all-to-all-done.1 = bf16[64,2,2048]{2,1,0:T(2,128)(2,1)} async-done(((bf16[64,2,2048]{2,1,0:T(2,128)(2,1)}), bf16[64,2,2048]{2,1,0:T(2,128)(2,1)}, u32[]{:S(2)}, u32[]{:S(2)}) %all-to-all-start.1) | async-done | bytes 524320 | tf_op jit(solution)/shard_map/all_to_all | solution.py:41
  72.9 2.5 %fusion.48 = f32[128,64]{0,1:T(8,128)S(1)} fusion(bf16[128,2048,1]{1,0,2:T(8,128)(2,1)} %reshape.206, bf16[2048,8,64]{0,2,1:T(8,128)(2,1)} %param.13, f32[128,8]{0,1:T(8,128)S(1)} %get-tuple-element.10), kind=kOutput, calls=%fused_computation.39 | convolution fusion | flops 268558336 | bytes 2658304 | tf_op jit(solution)/shard_map/dot_general | solution.py:11
  75.4 14.3 %all-reduce = (bf16[128,64]{0,1:T(8,128)(2,1)}, bf16[128,64]{0,1:T(8,128)(2,1)S(1)}) all-reduce(f32[128,64]{0,1:T(8,128)S(1)} %fusion.45, f32[128,64]{0,1:T(8,128)S(1)} %fusion.48), channel_id=1, replica_groups=mesh['pool'=64,'tp'=4] {'tp'}, use_global_device_ids=true, to_apply=%region_7.8 | all-reduce | flops 16384 | bytes 98304 | tf_op jit(solution)/shard_map/psum | solution.py:47
  89.7 2.9 %fusion.10 = bf16[128,2048]{1,0:T(8,128)(2,1)} fusion(bf16[8,64,2048]{2,1,0:T(8,128)(2,1)} %param.14, bf16[128,64]{0,1:T(8,128)(2,1)S(1)} %get-tuple-element.6, bf16[128,8]{0,1:T(8,128)(2,1)S(1)} %get-tuple-element.9), kind=kOutput, calls=%fused_computation.14 | convolution fusion | flops 269025280 | bytes 2639872 | tf_op jit(solution)/shard_map/dot_general | solution.py:23
  92.6 2.2 %all_to_all.44 = bf16[64,2,2048]{2,1,0:T(2,128)(2,1)} reshape(bf16[128,2048]{1,0:T(8,128)(2,1)} %fusion.10) | data formatting | bytes 1048576 | tf_op jit(solution)/shard_map/all_to_all | solution.py:49
  94.8 10.2 %all-to-all-start.2 = ((bf16[64,2,2048]{2,1,0:T(2,128)(2,1)}), bf16[64,2,2048]{2,1,0:T(2,128)(2,1)}, u32[]{:S(2)}, u32[]{:S(2)}) async-start(bf16[64,2,2048]{2,1,0:T(2,128)(2,1)} %all_to_all.44), calls=%async_computation.2 | async-start | bytes 1048576 | tf_op jit(solution)/shard_map/all_to_all | solution.py:49
  105.0 11.1 %gather_fusion = bf16[192,32,2,128]{3,2,1,0:T(2,128)(2,1)} fusion(bf16[192,32,2,128]{3,2,1,0:T(2,128)(2,1)S(1)} %copy-done, s32[1024]{0:T(1024)S(1)} %pad_clamp_fusion), kind=kCustom, calls=%fused_computation | custom fusion | bytes 6292224 | tf_op jit(solution)/shard_map/gather | solution.py:125
  116.1 12.9 %gather_fusion.1 = bf16[192,32,2,128]{3,2,1,0:T(2,128)(2,1)} fusion(bf16[192,32,2,128]{3,2,1,0:T(2,128)(2,1)} %param.17, s32[1024]{0:T(1024)S(1)} %pad_clamp_fusion), kind=kCustom, calls=%fused_computation.1 | custom fusion | bytes 6292224 | tf_op jit(solution)/shard_map/gather | solution.py:126
  132.6 2.9 %fusion.11 = bf16[128,2048]{1,0:T(8,128)(2,1)} fusion(bf16[8,64,2048]{2,1,0:T(8,128)(2,1)} %param.14, bf16[128,64]{0,1:T(8,128)(2,1)} %get-tuple-element.5, bf16[128,8]{0,1:T(8,128)(2,1)S(1)} %get-tuple-element.9), kind=kOutput, calls=%fused_computation.15 | convolution fusion | flops 269025280 | bytes 2639872 | tf_op jit(solution)/shard_map/dot_general | solution.py:23
  135.5 2.2 %all_to_all.50 = bf16[64,2,2048]{2,1,0:T(2,128)(2,1)} reshape(bf16[128,2048]{1,0:T(8,128)(2,1)} %fusion.11) | data formatting | bytes 1048576 | tf_op jit(solution)/shard_map/all_to_all | solution.py:49
  137.7 10.5 %all-to-all-start.4 = ((bf16[64,2,2048]{2,1,0:T(2,128)(2,1)}), bf16[64,2,2048]{2,1,0:T(2,128)(2,1)}, u32[]{:S(2)}, u32[]{:S(2)}) async-start(bf16[64,2,2048]{2,1,0:T(2,128)(2,1)} %all_to_all.50), calls=%async_computation.4 | async-start | bytes 1048576 | tf_op jit(solution)/shard_map/all_to_all | solution.py:49
  152.3 4.3 %fusion.86 = (f32[48,2,8]{2,1,0:T(2,128)}, f32[48,2,8,128]{3,2,1,0:T(8,128)S(1)}) fusion(bf16[48,2,8,128]{3,2,1,0:T(8,128)(2,1)S(1)} %bitcast.97, bf16[48,128,2,128]{3,2,1,0:T(2,128)(2,1)} %bitcast.91, pred[48,128]{1,0:T(8,128)(4,1)S(1)} %iota_compare_fusion.6), kind=kOutput, calls=%fused_computation.102 | convolution fusion | flops 25459968 | bytes 3744768 | tf_op jit(solution)/shard_map/rkgh,rtkh->rkgt/dot_general | solution.py:57
  169.5 3.7 %fusion.33 = bf16[48,2,8,128]{3,2,1,0:T(8,128)(2,1)} fusion(bf16[48,128,2,128]{3,2,1,0:T(2,128)(2,1)} %bitcast.93, f32[48,2,8,128]{3,2,1,0:T(8,128)S(1)} %get-tuple-element.18, f32[48,2,128]{2,1,0:T(2,128)} %bitcast_convert_fusion, f32[48,2,8]{2,1,0:T(2,128)} %copy.62, f32[48,2,8]{2,1,0:T(2,128)} %copy.60, f32[48,2,8]{2,1,0:T(2,128)} %copy.58), kind=kOutput, calls=%fused_computation.32 | convolution fusion | flops 25755648 | bytes 3793920 | tf_op jit(solution)/shard_map/rkgt,rtkh->rkgh/dot_general | solution.py:69
  177.8 3.7 %fusion.84 = (f32[48,2,8]{2,1,0:T(2,128)S(1)}, f32[48,2,8,128]{3,2,1,0:T(8,128)S(1)}) fusion(bf16[48,2,8,128]{3,2,1,0:T(8,128)(2,1)S(1)} %bitcast.95, bf16[48,128,2,128]{3,2,1,0:T(2,128)(2,1)} %bitcast.92, pred[48,128]{1,0:T(8,128)(4,1)S(1)} %copy-done.5), kind=kOutput, calls=%fused_computation.100 | convolution fusion | flops 25459968 | bytes 3744768 | tf_op jit(solution)/shard_map/rkgh,rtkh->rkgt/dot_general | solution.py:57
  (68 shorter events, 37.3 us)
Async XLA Ops:
  0.0 105.0 %copy-start = (bf16[192,32,2,128]{3,2,1,0:T(2,128)(2,1)S(1)}, bf16[192,32,2,128]{3,2,1,0:T(2,128)(2,1)}, u32[]{:S(2)}) copy-start(bf16[192,32,2,128]{3,2,1,0:T(2,128)(2,1)} %param.16) | copy-start | bytes 9437188
  0.0 53.6 %copy-start.10 = (s32[48,4]{0,1:T(4,128)S(1)}, s32[48,4]{0,1:T(4,128)}, u32[]{:S(2)}) copy-start(s32[48,4]{0,1:T(4,128)} %param.20) | copy-start | bytes 2308
  1.0 149.2 %copy-start.8 = (s32[48]{0:T(128)}, s32[48]{0:T(128)S(1)}, u32[]{:S(2)}) copy-start(s32[48]{0:T(128)S(1)} %multiply_add_fusion) | copy-start | bytes 580
  1.9 22.4 %all-to-all-start = ((s32[64,2,1]{1,2,0:T(1,128)}), s32[64,2,1]{1,2,0:T(1,128)S(1)}, u32[]{:S(2)}, u32[]{:S(2)}) async-start(s32[64,2,1]{1,2,0:T(1,128)} %bitcast.1), calls=%async_computation | async-start | bytes 65536 | tf_op jit(solution)/shard_map/all_to_all | solution.py:42
  24.3 22.9 %all-to-all-start.3 = ((bf16[64,2,2048]{2,1,0:T(2,128)(2,1)}), bf16[64,2,2048]{2,1,0:T(2,128)(2,1)}, u32[]{:S(2)}, u32[]{:S(2)}) async-start(bf16[64,2,2048]{2,1,0:T(2,128)(2,1)} %all_to_all.47), calls=%async_computation.3 | async-start | bytes 1048576 | tf_op jit(solution)/shard_map/all_to_all | solution.py:41
  47.1 23.7 %all-to-all-start.1 = ((bf16[64,2,2048]{2,1,0:T(2,128)(2,1)}), bf16[64,2,2048]{2,1,0:T(2,128)(2,1)}, u32[]{:S(2)}, u32[]{:S(2)}) async-start(bf16[64,2,2048]{2,1,0:T(2,128)(2,1)} %all_to_all.41), calls=%async_computation.1 | async-start | bytes 1048576 | tf_op jit(solution)/shard_map/all_to_all | solution.py:41
  94.8 42.9 %all-to-all-start.2 = ((bf16[64,2,2048]{2,1,0:T(2,128)(2,1)}), bf16[64,2,2048]{2,1,0:T(2,128)(2,1)}, u32[]{:S(2)}, u32[]{:S(2)}) async-start(bf16[64,2,2048]{2,1,0:T(2,128)(2,1)} %all_to_all.44), calls=%async_computation.2 | async-start | bytes 1048576 | tf_op jit(solution)/shard_map/all_to_all | solution.py:49
  129.1 21.2 %copy-start.3 = (bf16[2,48,2048]{2,1,0:T(8,128)(2,1)S(1)}, bf16[2,48,2048]{2,1,0:T(8,128)(2,1)}, u32[]{:S(2)}) copy-start(bf16[2,48,2048]{2,1,0:T(8,128)(2,1)} %param.12) | copy-start | bytes 1179652
  129.8 21.8 %copy-start.4 = (pred[48,128]{1,0:T(8,128)(4,1)}, pred[48,128]{1,0:T(8,128)(4,1)S(1)}, u32[]{:S(2)}) copy-start(pred[48,128]{1,0:T(8,128)(4,1)S(1)} %iota_compare_fusion.6) | copy-start | bytes 18436
  137.7 36.5 %all-to-all-start.4 = ((bf16[64,2,2048]{2,1,0:T(2,128)(2,1)}), bf16[64,2,2048]{2,1,0:T(2,128)(2,1)}, u32[]{:S(2)}, u32[]{:S(2)}) async-start(bf16[64,2,2048]{2,1,0:T(2,128)(2,1)} %all_to_all.50), calls=%async_computation.4 | async-start | bytes 1048576 | tf_op jit(solution)/shard_map/all_to_all | solution.py:49
  151.6 0.7 copy-start.2
  169.5 6.8 %copy-start.9 = (s32[48]{0:T(128)S(1)}, s32[48]{0:T(128)}, u32[]{:S(2)}) copy-start(s32[48]{0:T(128)} %copy-done.8) | copy-start | bytes 580
  169.5 8.3 %copy-start.5 = (pred[48,128]{1,0:T(8,128)(4,1)S(1)}, pred[48,128]{1,0:T(8,128)(4,1)}, u32[]{:S(2)}) copy-start(pred[48,128]{1,0:T(8,128)(4,1)} %copy-done.4) | copy-start | bytes 18436
  174.2 7.4 %copy-start.6 = (bf16[2,48,2,128]{3,2,1,0:T(2,128)(2,1)S(1)}, bf16[2,48,2,128]{3,2,1,0:T(2,128)(2,1)}, u32[]{:S(2)}) copy-start(bf16[2,48,2,128]{3,2,1,0:T(2,128)(2,1)} %param.18) | copy-start | bytes 147460
  176.2 6.3 %copy-start.1 = (bf16[192,32,2,128]{3,2,1,0:T(2,128)(2,1)S(1)}, bf16[192,32,2,128]{3,2,1,0:T(2,128)(2,1)}, u32[]{:S(2)}) copy-start(bf16[192,32,2,128]{3,2,1,0:T(2,128)(2,1)} %gather_fusion.1) | copy-start | bytes 9437188
  182.5 1.0 copy-start.7
where the time goes:
time: 188 us; the launch traced here: 186 us
  local copies, waits for them, and re-layouts  54.1 us (29%)
  starting transfers between devices  46 us (24%)
  matrix products  33.7 us (18%)
  waiting for transfers between devices  28.9 us (15%)
  blocking collectives  14.3 us (8%)
  other arithmetic  9.05 us (5%)
    all_to_all x2, waiting for transfers between devices, adapter_step_update(): lax.all_to_all(x_slots, 'pool', split_axis=0, concat_axis=0, tiled=True)  24 us
    all_to_all x2, starting transfers between devices, adapter_step_update(): lax.all_to_all(query_correction, 'pool', split_axis=0, concat_axis=0, til...  20.7 us
    psum x1, blocking collectives, adapter_step_update(): u_bf = lax.psum(u_part, 'tp').astype(jnp.bfloat16)  14.3 us
    all_to_all x1, starting transfers between devices, adapter_step_update(): lax.all_to_all(slot_index_list, 'pool', split_axis=0, concat_axis=0, tile...  13.2 us
    gather x1, local copies, waits for them, and re-layouts, shards(): values = paged_value_cache[row_page_table].reshape(rows, -1, kvn, head)  12.9 us
    all_to_all x2, starting transfers between devices, adapter_step_update(): lax.all_to_all(x_slots, 'pool', split_axis=0, concat_axis=0, tiled=True)  12.1 us
    gather x1, local copies, waits for them, and re-layouts, shards(): keys = paged_key_cache[row_page_table].reshape(rows, -1, kvn, head)  11.1 us
    all_to_all x4, local copies, waits for them, and re-layouts, adapter_step_update(): lax.all_to_all(query_correction, 'pool', split_axis=0, concat_axis=0, til...  8.48 us
  transfers between devices with their start and end apart: 5, of which 3 were waited for; matrix products, arithmetic and copies ran while one was open for 34% of the time, Pallas kernels for 0%

commit v1 on v0

v1 whole, which is shorter than its diff:
```python
import functools

import jax
import jax.numpy as jnp
from jax import lax
from jax.experimental import pallas as pl
from jax.experimental.pallas import tpu as pltpu
from jax.sharding import PartitionSpec as P

ADAPTER_SCALE = 0.5
MESH = pl.DeviceIdType.MESH
Y, Z, C = 4, 8, 2
POOL = Y * Z * C
TP = 4
GROUP = 8
GROUPS = POOL // GROUP
STEPS = 2
SLOTS = 2
PER = STEPS * SLOTS
BLOCK = 16
LANES = 128


def offsets(k):
    return k // (Z * C), k % Z, (k // Z) % C


def ahead(me, k):
    dy, dz, dc = offsets(k)
    y, z, c = me // (Z * C), (me // C) % Z, me % C
    return (((y + dy) % Y) * Z + (z + dz) % Z) * C + (c + dc) % C


def behind(me, k):
    dy, dz, dc = offsets(k)
    y, z, c = me // (Z * C), (me // C) % Z, me % C
    return (((y + Y - dy) % Y) * Z + (z + Z - dz) % Z) * C + (c + C - dc) % C


def position(me, other):
    y, z, c = me // (Z * C), (me // C) % Z, me % C
    oy, oz, oc = other // (Z * C), (other // C) % Z, other % C
    dy, dz, dc = (oy - y + Y) % Y, (oz - z + Z) % Z, (oc - c + C) % C
    return (dy * C + dc) * Z + dz


def kernel(
    rows,
    ctx,
    page,
    slot_row,
    row_answer,
    pages,
    lengths,
    picks,
    x_hbm,
    base_hbm,
    down_hbm,
    up_hbm,
    key_hbm,
    value_hbm,
    new_key_hbm,
    new_value_hbm,
    out_ref,
    x_in,
    base_in,
    down,
    up,
    keys,
    values,
    new_keys,
    new_values,
    x_blocks,
    base_blocks,
    out_blocks,
    sent,
    got,
    got_picks,
    masks,
    own_part,
    parts,
    wide,
    answers,
    returned,
    local_sems,
    x_send,
    x_recv,
    pick_send,
    pick_recv,
    part_send,
    part_recv,
    answer_send,
    answer_recv,
):
    me = lax.axis_index("pool")
    my_tp = lax.axis_index("tp")
    heads = BLOCK
    f32, bf16 = jnp.float32, jnp.bfloat16

    barrier = pltpu.get_barrier_semaphore()

    def greet(k, _):
        pl.semaphore_signal(
            barrier, inc=1, device_id={"pool": ahead(me, k)}, device_id_type=MESH
        )
        return 0

    lax.fori_loop(1, POOL, greet, 0)
    for t in range(1, TP):
        pl.semaphore_signal(
            barrier, inc=1, device_id={"tp": (my_tp + t) % TP}, device_id_type=MESH
        )

    loads = [
        pltpu.make_async_copy(src, dst, local_sems.at[i])
        for i, (src, dst) in enumerate(
            (
                (x_hbm, x_in),
                (down_hbm, down),
                (up_hbm, up),
                (base_hbm, base_in),
                (key_hbm, keys),
                (value_hbm, values),
                (new_key_hbm, new_keys),
                (new_value_hbm, new_values),
            )
        )
    ]
    for load in loads:
        load.start()

    def to_blocks(src, dst):
        for s in range(STEPS):
            for c in range(BLOCK):
                dst[pl.ds(s * rows * BLOCK + c, rows, stride=BLOCK), :] = src[
                    s, :, c * LANES : (c + 1) * LANES
                ].astype(f32)

    loads[0].wait()
    to_blocks(x_in, base_blocks)
    x_blocks[...] = base_blocks[...].astype(bf16).reshape(STEPS * rows, BLOCK, LANES)

    pl.semaphore_wait(barrier, POOL - 1 + TP - 1)

    def message(k, src, dst, send_sem, recv_sem, to):
        return pltpu.make_async_remote_copy(
            src_ref=src.at[pl.ds(k * PER, PER)],
            dst_ref=dst.at[pl.ds(k * PER, PER)],
            send_sem=send_sem,
            recv_sem=recv_sem,
            device_id={"pool": to},
            device_id_type=MESH,
        )

    def blocks_of(k, dst):
        for j in range(SLOTS):
            row = slot_row[k * SLOTS + j]
            for s in range(STEPS):
                dst[k * PER + s * SLOTS + j] = x_blocks[row + s * rows]

    def send_row(k, _):
        blocks_of(k, sent)
        to = ahead(me, k)
        pltpu.make_async_remote_copy(
            src_ref=picks.at[k],
            dst_ref=got_picks.at[k],
            send_sem=pick_send,
            recv_sem=pick_recv.at[k // GROUP],
            device_id={"pool": to},
            device_id_type=MESH,
        ).start()
        message(k, sent, got, x_send, x_recv.at[k // GROUP], to).start()
        return 0

    lax.fori_loop(1, POOL, send_row, 0)
    blocks_of(0, got)
    got_picks[0] = picks[0]

    loads[1].wait()
    loads[2].wait()

    grows = GROUP * PER
    width = down.shape[0]
    rank = width // 8
    spread = (
        lax.broadcasted_iota(jnp.int32, (grows, GROUP), 0) // PER
        == lax.broadcasted_iota(jnp.int32, (grows, GROUP), 1)
    ).astype(f32)
    lane = lax.broadcasted_iota(jnp.int32, (grows, LANES), 1)
    slot = lax.broadcasted_iota(jnp.int32, (grows, LANES), 0) % SLOTS
    slot_lanes = (lane // 8 == slot).astype(f32)
    widen = (
        lax.broadcasted_iota(jnp.int32, (LANES, width), 0) % 8
        == lax.broadcasted_iota(jnp.int32, (LANES, width), 1) // rank
    ).astype(f32)

    def group_bytes(g, first, ref, per, sem):
        lo, n = g * GROUP * per, GROUP * per
        if first:
            lo, n = per, (GROUP - 1) * per
        part = ref.at[pl.ds(lo, n)]
        pltpu.make_async_copy(part, part, sem).wait()

    def project_down(g, first):
        group_bytes(g, first, got, PER, x_recv.at[g])
        group_bytes(g, first, got_picks, 1, pick_recv.at[g])
        wide[...] = got[pl.ds(g * grows, grows)].reshape(grows * BLOCK, LANES).astype(f32)
        features = jnp.concatenate(
            [wide[pl.ds(c, grows, stride=BLOCK), :] for c in range(BLOCK)], axis=1
        ).astype(bf16)
        product = lax.dot_general(
            features, down[...], (((1,), (1,)), ((), ())), preferred_element_type=f32
        )
        chosen = got_picks[pl.ds(g * GROUP, GROUP)].reshape(GROUP, LANES)
        chosen = jnp.dot(spread, chosen, preferred_element_type=f32) * slot_lanes
        mask = jnp.dot(chosen, widen, preferred_element_type=f32)
        masks[g] = mask.astype(bf16)
        product = product * mask
        part = product[:, :LANES]
        for i in range(1, width // LANES):
            part = part + product[:, i * LANES : (i + 1) * LANES]
        own_part[g] = part
        for t in range(1, TP):
            pltpu.make_async_remote_copy(
                src_ref=own_part.at[g],
                dst_ref=parts.at[g, t - 1],
                send_sem=part_send,
                recv_sem=part_recv.at[g],
                device_id={"tp": (my_tp + t) % TP},
                device_id_type=MESH,
            ).start()

    def project_up(g, first):
        pltpu.make_async_copy(parts.at[g], parts.at[g], part_recv.at[g]).wait()
        u = own_part[g] + parts[g, 0] + parts[g, 1] + parts[g, 2]
        u = u.astype(bf16)
        u = jnp.concatenate([u] * (width // LANES), axis=1) * masks[g]
        delta = jnp.dot(u, up[...], preferred_element_type=f32) * ADAPTER_SCALE
        for c in range(BLOCK):
            wide[pl.ds(c, grows, stride=BLOCK), :] = delta[:, c * LANES : (c + 1) * LANES]
        answers[pl.ds(g * grows, grows)] = (
            wide[...].astype(bf16).reshape(grows, BLOCK, LANES)
        )

        def answer(k, _):
            message(k, answers, returned, answer_send, answer_recv, behind(me, k)).start()
            return 0

        if first:
            returned[pl.ds(0, PER)] = answers[pl.ds(0, PER)]
            lax.fori_loop(1, GROUP, answer, 0)
        else:
            lax.fori_loop(g * GROUP, (g + 1) * GROUP, answer, 0)

    project_down(0, True)
    project_down(1, False)
    project_up(0, True)

    def advance(g, _):
        project_down(g, False)
        project_up(g - 1, False)
        return 0

    lax.fori_loop(2, GROUPS, advance, 0)
    project_up(GROUPS - 1, False)

    for load in loads[3:]:
        load.wait()
    to_blocks(base_in, base_blocks)

    tail = returned.at[pl.ds(PER, (POOL - 1) * PER)]
    pltpu.make_async_copy(tail, tail, answer_recv).wait()

    kv = 2
    old = ctx * kv
    cols = old + STEPS * BLOCK
    near = BLOCK // kv
    shape = (STEPS * heads, cols)
    col = lax.broadcasted_iota(jnp.int32, shape, 1)
    query_row = lax.broadcasted_iota(jnp.int32, shape, 0)
    same_head = (query_row % heads) // (heads // kv) == col % kv
    fresh = col - old
    is_old = col < old
    reachable = fresh // BLOCK <= query_row // heads
    old_key = jnp.where(same_head & is_old, col, 1 << 20)
    fresh_key = jnp.where(same_head & ~is_old & reachable, (fresh % BLOCK) // kv, -1)
    inv = 1.0 / (LANES**0.5)
    per_row = ctx // page

    def one_row(r, tile, within):
        answer_at = row_answer[r]
        queries = []
        for s in range(STEPS):
            at = pl.multiple_of((s * rows + r) * BLOCK, BLOCK)
            delta = returned[answer_at + s * SLOTS].astype(f32)
            queries.append((base_blocks[pl.ds(at, BLOCK), :] + delta).astype(bf16))
        query = jnp.concatenate(queries, axis=0)
        ids = [pages[r * per_row + i] for i in range(per_row)]
        fresh_at = [
            pl.ds(pl.multiple_of(s * rows * kv + tile * BLOCK, BLOCK), BLOCK)
            for s in range(STEPS)
        ]
        key = jnp.concatenate(
            [keys[i] for i in ids] + [new_keys[at, :] for at in fresh_at], axis=0
        )
        value = jnp.concatenate(
            [values[i] for i in ids] + [new_values[at, :] for at in fresh_at], axis=0
        )
        scores = (
            lax.dot_general(query, key, (((1,), (1,)), ((), ())), preferred_element_type=f32) * inv
        )
        live = (old_key < lengths[r] * kv) | (fresh_key == within)
        scores = jnp.where(live, scores, -1e30)
        top = jnp.max(scores, axis=-1, keepdims=True)
        e = jnp.exp(scores - top)
        weights = (e / jnp.sum(e, axis=-1, keepdims=True)).astype(bf16)
        result = jnp.dot(weights, value, preferred_element_type=f32)
        for s in range(STEPS):
            at = pl.multiple_of((s * rows + r) * BLOCK, BLOCK)
            out_blocks[pl.ds(at, BLOCK), :] = result[s * heads : (s + 1) * heads]

    def eight_rows(tile, _):
        for within in range(near):
            one_row(tile * near + within, tile, within)
        return 0

    lax.fori_loop(0, rows // near, eight_rows, 0)

    for s in range(STEPS):
        for c in range(BLOCK):
            out_ref[s, :, c * LANES : (c + 1) * LANES] = out_blocks[
                pl.ds(s * rows * BLOCK + c, rows, stride=BLOCK), :
            ].astype(bf16)

    others = sent.at[pl.ds(PER, (POOL - 1) * PER)]
    pltpu.make_async_copy(others, others, x_send).wait()
    others = answers.at[pl.ds(PER, (POOL - 1) * PER)]
    pltpu.make_async_copy(others, others, answer_send).wait()
    others = got_picks.at[pl.ds(1, POOL - 1)]
    pltpu.make_async_copy(others, others, pick_send).wait()
    pltpu.make_async_copy(parts, parts, part_send).wait()


def shards(
    normed_input,
    base_query_output,
    adapter_down_weight,
    adapter_up_weight,
    row_adapter_index,
    paged_key_cache,
    paged_value_cache,
    step_token_keys,
    step_token_values,
    row_page_table,
    lengths,
):
    rows = row_adapter_index.shape[0]
    features = normed_input.shape[2]
    held, rank = adapter_up_weight.shape[:2]
    count, page, kv, head = paged_key_cache.shape
    ctx = page * row_page_table.shape[1]
    me = lax.axis_index("pool")

    owner = row_adapter_index // held
    local = row_adapter_index % held
    order = jnp.arange(rows, dtype=jnp.int32)
    earlier = jnp.sum(
        ((owner[None, :] == owner[:, None]) & (order[None, :] < order[:, None])).astype(jnp.int32),
        axis=1,
    )
    row_slot = position(me, owner) * SLOTS + earlier
    place = jnp.arange(POOL * SLOTS, dtype=jnp.int32)[:, None] == row_slot[None, :]
    slot_row = jnp.sum(jnp.where(place, order[None, :], 0), axis=1)
    lane = jnp.arange(LANES, dtype=jnp.int32)
    wanted = (row_slot[:, None] % SLOTS) * held + local[:, None] == lane[None, :]
    toward = jnp.arange(POOL, dtype=jnp.int32)[:, None] == row_slot[None, :] // SLOTS
    picks = jnp.sum(
        (toward[:, :, None] & wanted[None, :, :]).astype(jnp.float32), axis=1
    ).reshape(POOL, 1, LANES)

    bf16, f32 = jnp.bfloat16, jnp.float32
    smem = pl.BlockSpec(memory_space=pltpu.SMEM)
    vmem = pl.BlockSpec(memory_space=pltpu.VMEM)
    anywhere = pl.BlockSpec(memory_space=pl.ANY)
    dma = pltpu.SemaphoreType.DMA
    grows = GROUP * PER
    width = held * rank
    return pl.pallas_call(
        functools.partial(kernel, rows, ctx, page),
        out_shape=jax.ShapeDtypeStruct((STEPS, rows, features), bf16),
        in_specs=[smem] * 4 + [vmem] + [anywhere] * 8,
        out_specs=vmem,
        scratch_shapes=[
            pltpu.VMEM((STEPS, rows, features), bf16),
            pltpu.VMEM((STEPS, rows, features), bf16),
            pltpu.VMEM((width, features), bf16),
            pltpu.VMEM((width, features), bf16),
            pltpu.VMEM((count, page * kv, head), bf16),
            pltpu.VMEM((count, page * kv, head), bf16),
            pltpu.VMEM((STEPS * rows * kv, head), bf16),
            pltpu.VMEM((STEPS * rows * kv, head), bf16),
            pltpu.VMEM((STEPS * rows, BLOCK, LANES), bf16),
            pltpu.VMEM((STEPS * rows * BLOCK, LANES), f32),
            pltpu.VMEM((STEPS * rows * BLOCK, LANES), f32),
            pltpu.VMEM((POOL * PER, BLOCK, LANES), bf16),
            pltpu.VMEM((POOL * PER, BLOCK, LANES), bf16),
            pltpu.VMEM((POOL, 1, LANES), f32),
            pltpu.VMEM((GROUPS, grows, width), bf16),
            pltpu.VMEM((GROUPS, grows, LANES), f32),
            pltpu.VMEM((GROUPS, TP - 1, grows, LANES), f32),
            pltpu.VMEM((grows * BLOCK, LANES), f32),
            pltpu.VMEM((POOL * PER, BLOCK, LANES), bf16),
            pltpu.VMEM((POOL * PER, BLOCK, LANES), bf16),
            dma((8,)),
            dma,
            dma((GROUPS,)),
            dma,
            dma((GROUPS,)),
            dma,
            dma((GROUPS,)),
            dma,
            dma,
        ],
        compiler_params=pltpu.CompilerParams(
            collective_id=0, has_side_effects=True, vmem_limit_bytes=60 << 20
        ),
        cost_estimate=pl.CostEstimate(
            flops=3_000_000_000, bytes_accessed=12_000_000, transcendentals=1_000_000
        ),
        name="adapters_and_attention",
    )(
        slot_row,
        row_slot // SLOTS * PER + row_slot % SLOTS,
        row_page_table.reshape(-1),
        lengths,
        picks,
        normed_input,
        base_query_output,
        adapter_down_weight.transpose(1, 2, 0).reshape(width, features),
        adapter_up_weight.reshape(width, features),
        paged_key_cache.reshape(count, page * kv, head),
        paged_value_cache.reshape(count, page * kv, head),
        step_token_keys.reshape(STEPS * rows * kv, head),
        step_token_values.reshape(STEPS * rows * kv, head),
    )


def solution(mesh):
    placed = (
        P(None, "pool", "tp"),
        P(None, "pool", "tp"),
        P("tp", "pool", None),
        P("pool", None, "tp"),
        P("pool"),
        P("pool", None, "tp", None),
        P("pool", None, "tp", None),
        P(None, "pool", "tp", None),
        P(None, "pool", "tp", None),
        P("pool", None),
        P("pool"),
    )
    return jax.shard_map(
        shards, mesh=mesh, in_specs=placed, out_specs=P(None, "pool", "tp"), check_vma=False
    )
```

time: 188 us -> 86.3 us (0.46)
  Pallas kernels: 0 us -> 78.8 us
  local copies, waits for them, and re-layouts: 54.1 us -> 3.21 us
  starting transfers between devices: 46 us -> 0 us
  matrix products: 33.7 us -> 0 us
  waiting for transfers between devices: 28.9 us -> 0 us
  blocking collectives: 14.3 us -> 0 us
  other arithmetic: 9.05 us -> 4.08 us
    pallas_call x0 -> x1, Pallas kernels: none -> 78.8 us  [shards(): pl.pallas_call(functools.partial(kernel, rows, ctx, page), out_shape=jax....]
    all_to_all x5 -> x0, starting transfers between devices: 46 us -> none  [the longest x2 20.7 us: adapter_step_update(): lax.all_to_all(query_correction, 'pool', split_axis=0, concat_axis=0, til...]
    dot_general x15 -> x0, matrix products: 33.7 us -> none  [the longest x2 8.07 us: attend_all(): jnp.einsum('rkgh,rtkh->rkgt', grouped, keys, preferred_element_type=jnp.f...]
    all_to_all x5 -> x0, waiting for transfers between devices: 28.9 us -> none  [the longest x2 24 us: adapter_step_update(): lax.all_to_all(x_slots, 'pool', split_axis=0, concat_axis=0, tiled=True)]
    gather x2 -> x0, local copies, waits for them, and re-layouts: 24 us -> none  [the longest x1 12.9 us: shards(): values = paged_value_cache[row_page_table].reshape(rows, -1, kvn, head)]
    all_to_all x10 -> x0, local copies, waits for them, and re-layouts: 18.2 us -> none  [the longest x4 8.48 us: adapter_step_update(): lax.all_to_all(query_correction, 'pool', split_axis=0, concat_axis=0, til...]
    psum x1 -> x0, blocking collectives: 14.3 us -> none  [adapter_step_update(): u_bf = lax.psum(u_part, 'tp').astype(jnp.bfloat16)]
    another operation x2 -> x0, other arithmetic: 2.15 us -> none
  transfers between devices with their start and end apart: 5 -> 0, of which waited for: 3 -> 0; matrix products, arithmetic and copies ran while one was open for 34% -> 0% of each run, Pallas kernels for 0% -> 0%
where the time goes in v1:
time: 86.3 us; the launch traced here: 86.1 us
  Pallas kernels  78.8 us (91%)
  other arithmetic  4.08 us (5%)
  local copies, waits for them, and re-layouts  3.21 us (4%)
    pallas_call x1, Pallas kernels, shards(): pl.pallas_call(functools.partial(kernel, rows, ctx, page), out_shape=jax....  78.8 us
    unnamed x2, local copies, waits for them, and re-layouts  2.53 us

profile of v1, /device:TPU:1, one launch (start us, length us, event | category | flops | bytes accessed | tf_op | source)
XLA Modules:
  0.0 86.1 jit_solution(16731862660767631809)
XLA Ops:
  0.0 0.7 and_select_fusion.10
  0.7 0.2 convert_reduce_fusion.1
  0.8 0.7 fusion.3
  1.6 0.6 select_reduce_fusion.slot_row
  2.2 0.6 multiply_add_fusion
  2.8 0.1 iota_compare_fusion.1
  2.9 1.2 %convert_reduce_fusion = f32[64,128]{1,0:T(8,128)} fusion(pred[48,128]{1,0:T(8,128)(4,1)S(1)} %iota_compare_fusion.1, pred[64,48]{1,0:T(8,128)(4,1)S(1)} %iota_compare_fusion), kind=kLoop, calls=%fused_computation | loop fusion | flops 1171456 | bytes 41984 | tf_op jit(solution)/shard_map/reduce_sum | solution.py:377
  4.1 0.8 copy.13
  4.9 0.7 reshape.89.pages
  5.5 78.8 %adapters_and_attention.1 = bf16[2,48,2048]{2,1,0:T(8,128)(2,1)} custom-call(s32[128]{0:T(128)} %select_reduce_fusion.slot_row, s32[48]{0:T(128)} %get-tuple-element.8.row_answer, s32[192]{0:T(256)} %reshape.89.pages, s32[48]{0:T(128)} %lengths.1, f32[64,1,128]{2,1,0:T(1,128)} %bitcast.13, bf16[2,48,2048]{2,1,0:T(8,128)(2,1)} %x_hbm.1, ...), custom_call_target="tpu_custom_call" | custom-call | flops 3000000000 | bytes 12000000 | tf_op jit(solution)/shard_map/adapters_and_attention/pallas_call | solution.py:388
  84.3 1.8 %copy.15 = bf16[2,48,2048]{2,1,0:T(8,128)(2,1)} copy(bf16[2,48,2048]{2,1,0:T(8,128)(2,1)} %adapters_and_attention.1) | data formatting | bytes 786432
  (1 shorter events, 0.0 us)

commit v2 on v1

--- a/solution.py
+++ b/solution.py
@@ -8,6 +8,7 @@
 from jax.sharding import PartitionSpec as P
 
 ADAPTER_SCALE = 0.5
+LOG2_E = 1.4426950408889634
 MESH = pl.DeviceIdType.MESH
 Y, Z, C = 4, 8, 2
 POOL = Y * Z * C
@@ -273,55 +274,68 @@
 
     kv = 2
     old = ctx * kv
-    cols = old + STEPS * BLOCK
     near = BLOCK // kv
-    shape = (STEPS * heads, cols)
+    mine = STEPS * heads
+    col = lax.broadcasted_iota(jnp.int32, (mine, old), 1)
+    query_row = lax.broadcasted_iota(jnp.int32, (mine, old), 0)
+    old_key = jnp.where((query_row % heads) // (heads // kv) == col % kv, col, 1 << 20)
+    shape = (near * mine, STEPS * BLOCK)
     col = lax.broadcasted_iota(jnp.int32, shape, 1)
     query_row = lax.broadcasted_iota(jnp.int32, shape, 0)
-    same_head = (query_row % heads) // (heads // kv) == col % kv
-    fresh = col - old
-    is_old = col < old
-    reachable = fresh // BLOCK <= query_row // heads
-    old_key = jnp.where(same_head & is_old, col, 1 << 20)
-    fresh_key = jnp.where(same_head & ~is_old & reachable, (fresh % BLOCK) // kv, -1)
-    inv = 1.0 / (LANES**0.5)
+    fresh_live = (
+        ((col % BLOCK) // kv == query_row // mine)
+        & (col // BLOCK <= (query_row % mine) // heads)
+        & (col % kv == (query_row % heads) // (heads // kv))
+    )
     per_row = ctx // page
-
-    def one_row(r, tile, within):
-        answer_at = row_answer[r]
+    scale = LOG2_E / (LANES**0.5)
+
+    def eight_rows(tile, _):
         queries = []
-        for s in range(STEPS):
-            at = pl.multiple_of((s * rows + r) * BLOCK, BLOCK)
-            delta = returned[answer_at + s * SLOTS].astype(f32)
-            queries.append((base_blocks[pl.ds(at, BLOCK), :] + delta).astype(bf16))
+        for i in range(near):
+            r = tile * near + i
+            for s in range(STEPS):
+                at = pl.multiple_of((s * rows + r) * BLOCK, BLOCK)
+                delta = returned[row_answer[r] + s * SLOTS].astype(f32)
+                queries.append((base_blocks[pl.ds(at, BLOCK), :] + delta).astype(bf16))
         query = jnp.concatenate(queries, axis=0)
-        ids = [pages[r * per_row + i] for i in range(per_row)]
         fresh_at = [
             pl.ds(pl.multiple_of(s * rows * kv + tile * BLOCK, BLOCK), BLOCK)
             for s in range(STEPS)
         ]
-        key = jnp.concatenate(
-            [keys[i] for i in ids] + [new_keys[at, :] for at in fresh_at], axis=0
-        )
-        value = jnp.concatenate(
-            [values[i] for i in ids] + [new_values[at, :] for at in fresh_at], axis=0
-        )
-        scores = (
-            lax.dot_general(query, key, (((1,), (1,)), ((), ())), preferred_element_type=f32) * inv
-        )
-        live = (old_key < lengths[r] * kv) | (fresh_key == within)
-        scores = jnp.where(live, scores, -1e30)
-        top = jnp.max(scores, axis=-1, keepdims=True)
-        e = jnp.exp(scores - top)
-        weights = (e / jnp.sum(e, axis=-1, keepdims=True)).astype(bf16)
-        result = jnp.dot(weights, value, preferred_element_type=f32)
-        for s in range(STEPS):
-            at = pl.multiple_of((s * rows + r) * BLOCK, BLOCK)
-            out_blocks[pl.ds(at, BLOCK), :] = result[s * heads : (s + 1) * heads]
-
-    def eight_rows(tile, _):
-        for within in range(near):
-            one_row(tile * near + within, tile, within)
+        new_key = jnp.concatenate([new_keys[at, :] for at in fresh_at], axis=0)
+        new_value = jnp.concatenate([new_values[at, :] for at in fresh_at], axis=0)
+        transposed = (((1,), (1,)), ((), ()))
+        fresh = lax.dot_general(query, new_key, transposed, preferred_element_type=f32)
+        fresh = jnp.where(fresh_live, fresh, -1e30)
+        scores = []
+        for i in range(near):
+            r = tile * near + i
+            key = jnp.concatenate([keys[pages[p, r]] for p in range(per_row)], axis=0)
+            part = lax.dot_general(
+                query[i * mine : (i + 1) * mine], key, transposed, preferred_element_type=f32
+            )
+            scores.append(jnp.where(old_key < lengths[r] * kv, part, -1e30))
+        scores = jnp.concatenate(scores, axis=0)
+        top = jnp.maximum(
+            jnp.max(scores, axis=-1, keepdims=True), jnp.max(fresh, axis=-1, keepdims=True)
+        )
+        e_old = jnp.exp2((scores - top) * scale)
+        e_new = jnp.exp2((fresh - top) * scale)
+        total = jnp.sum(e_old, axis=-1, keepdims=True) + jnp.sum(e_new, axis=-1, keepdims=True)
+        share = 1.0 / total
+        w_old = (e_old * share).astype(bf16)
+        w_new = (e_new * share).astype(bf16)
+        result = jnp.dot(w_new, new_value, preferred_element_type=f32)
+        for i in range(near):
+            r = tile * near + i
+            value = jnp.concatenate([values[pages[p, r]] for p in range(per_row)], axis=0)
+            both = result[i * mine : (i + 1) * mine] + jnp.dot(
+                w_old[i * mine : (i + 1) * mine], value, preferred_element_type=f32
+            )
+            for s in range(STEPS):
+                at = pl.multiple_of((s * rows + r) * BLOCK, BLOCK)
+                out_blocks[pl.ds(at, BLOCK), :] = both[s * heads : (s + 1) * heads]
         return 0
 
     lax.fori_loop(0, rows // near, eight_rows, 0)
@@ -431,7 +445,7 @@
     )(
         slot_row,
         row_slot // SLOTS * PER + row_slot % SLOTS,
-        row_page_table.reshape(-1),
+        row_page_table.T,
         lengths,
         picks,
         normed_input,

time: 86.3 us -> 73.3 us (0.85)
  Pallas kernels: 78.8 us -> 67.2 us
  local copies, waits for them, and re-layouts: 3.21 us -> 1.77 us
    pallas_call x1, Pallas kernels: 78.8 us -> 67.2 us  [shards(): pl.pallas_call(functools.partial(kernel, rows, ctx, page), out_shape=jax....]
    unnamed x2 -> x1, local copies, waits for them, and re-layouts: 2.53 us -> 1.77 us
where the time goes in v2:
time: 73.3 us; the launch traced here: 73.1 us
  Pallas kernels  67.2 us (92%)
  other arithmetic  4.06 us (6%)
  local copies, waits for them, and re-layouts  1.77 us (2%)
    pallas_call x1, Pallas kernels, shards(): pl.pallas_call(functools.partial(kernel, rows, ctx, page), out_shape=jax....  67.2 us
    unnamed x1, local copies, waits for them, and re-layouts  1.77 us

profile of v2, /device:TPU:1, one launch (start us, length us, event | category | flops | bytes accessed | tf_op | source)
XLA Modules:
  0.0 73.1 jit_solution(10438553548914636830)
XLA Ops:
  0.0 0.7 and_select_fusion.10
  0.7 0.2 convert_reduce_fusion.1
  0.8 0.7 fusion.3
  1.6 0.7 select_reduce_fusion.slot_row
  2.2 0.5 multiply_add_fusion
  2.7 0.1 iota_compare_fusion.1
  2.8 1.2 %convert_reduce_fusion = f32[64,128]{1,0:T(8,128)} fusion(pred[48,128]{1,0:T(8,128)(4,1)S(1)} %iota_compare_fusion.1, pred[64,48]{1,0:T(8,128)(4,1)S(1)} %iota_compare_fusion), kind=kLoop, calls=%fused_computation | loop fusion | flops 1171456 | bytes 41984 | tf_op jit(solution)/shard_map/reduce_sum | solution.py:391
  4.1 67.2 %adapters_and_attention.1 = bf16[2,48,2048]{2,1,0:T(8,128)(2,1)} custom-call(s32[128]{0:T(128)} %select_reduce_fusion.slot_row, s32[48]{0:T(128)} %get-tuple-element.8.row_answer, s32[4,48]{1,0:T(4,128)} %bitcast.17, s32[48]{0:T(128)} %lengths.1, f32[64,1,128]{2,1,0:T(1,128)} %bitcast.14, bf16[2,48,2048]{2,1,0:T(8,128)(2,1)} %x_hbm.1, ...), custom_call_target="tpu_custom_call" | custom-call | flops 3000000000 | bytes 12000000 | tf_op jit(solution)/shard_map/adapters_and_attention/pallas_call | solution.py:402
  71.3 1.8 %copy.13 = bf16[2,48,2048]{2,1,0:T(8,128)(2,1)} copy(bf16[2,48,2048]{2,1,0:T(8,128)(2,1)} %adapters_and_attention.1) | data formatting | bytes 786432
  (1 shorter events, 0.0 us)

commit v3 on v1

v3 whole, which is shorter than its diff:
```python
import functools

import jax
import jax.numpy as jnp
from jax import lax
from jax.experimental import pallas as pl
from jax.experimental.pallas import tpu as pltpu
from jax.sharding import PartitionSpec as P

ADAPTER_SCALE = 0.5
LOG2_E = 1.4426950408889634
MESH = pl.DeviceIdType.MESH
Y, Z, C = 4, 8, 2
POOL = Y * Z * C
TP = 4
GROUP = 8
GROUPS = POOL // GROUP
BATCH = 16
BATCHES = POOL // BATCH
THREE = 3
STEPS = 2
SLOTS = 2
PER = STEPS * SLOTS
BLOCK = 16
LANES = 128


def offsets(k):
    return k // (Z * C), k % Z, (k // Z) % C


def ahead(me, k):
    dy, dz, dc = offsets(k)
    y, z, c = me // (Z * C), (me // C) % Z, me % C
    return (((y + dy) % Y) * Z + (z + dz) % Z) * C + (c + dc) % C


def behind(me, k):
    dy, dz, dc = offsets(k)
    y, z, c = me // (Z * C), (me // C) % Z, me % C
    return (((y + Y - dy) % Y) * Z + (z + Z - dz) % Z) * C + (c + C - dc) % C


def position(me, other):
    y, z, c = me // (Z * C), (me // C) % Z, me % C
    oy, oz, oc = other // (Z * C), (other // C) % Z, other % C
    dy, dz, dc = (oy - y + Y) % Y, (oz - z + Z) % Z, (oc - c + C) % C
    return (dy * C + dc) * Z + dz


def greet_all(me, my_tp):
    barrier = pltpu.get_barrier_semaphore()

    def greet(k, _):
        pl.semaphore_signal(
            barrier, inc=1, device_id={"pool": ahead(me, k)}, device_id_type=MESH
        )
        return 0

    lax.fori_loop(1, POOL, greet, 0)
    for t in range(1, TP):
        pl.semaphore_signal(
            barrier, inc=1, device_id={"tp": (my_tp + t) % TP}, device_id_type=MESH
        )
    return barrier


def start_loads(pairs, sems):
    loads = [pltpu.make_async_copy(src, dst, sems.at[i]) for i, (src, dst) in enumerate(pairs)]
    for load in loads:
        load.start()
    return loads


def to_blocks(rows, src, dst):
    for s in range(STEPS):
        for c in range(BLOCK):
            dst[pl.ds(s * rows * BLOCK + c, rows, stride=BLOCK), :] = src[
                s, :, c * LANES : (c + 1) * LANES
            ].astype(jnp.float32)


def await_bytes(ref, sem):
    pltpu.make_async_copy(ref, ref, sem).wait()


def attend(
    rows,
    ctx,
    page,
    row_answer,
    pages,
    lengths,
    keys,
    values,
    new_keys,
    new_values,
    base_blocks,
    returned,
    out_blocks,
    out_ref,
):
    heads = BLOCK
    f32, bf16 = jnp.float32, jnp.bfloat16
    kv = 2
    old = ctx * kv
    near = BLOCK // kv
    mine = STEPS * heads
    col = lax.broadcasted_iota(jnp.int32, (mine, old), 1)
    query_row = lax.broadcasted_iota(jnp.int32, (mine, old), 0)
    old_key = jnp.where((query_row % heads) // (heads // kv) == col % kv, col, 1 << 20)
    shape = (near * mine, STEPS * BLOCK)
    col = lax.broadcasted_iota(jnp.int32, shape, 1)
    query_row = lax.broadcasted_iota(jnp.int32, shape, 0)
    fresh_live = (
        ((col % BLOCK) // kv == query_row // mine)
        & (col // BLOCK <= (query_row % mine) // heads)
        & (col % kv == (query_row % heads) // (heads // kv))
    )
    per_row = ctx // page
    scale = LOG2_E / (LANES**0.5)

    def eight_rows(tile, _):
        queries = []
        for i in range(near):
            r = tile * near + i
            for s in range(STEPS):
                at = pl.multiple_of((s * rows + r) * BLOCK, BLOCK)
                delta = returned[row_answer[s, r]].astype(f32)
                queries.append((base_blocks[pl.ds(at, BLOCK), :] + delta).astype(bf16))
        query = jnp.concatenate(queries, axis=0)
        fresh_at = [
            pl.ds(pl.multiple_of(s * rows * kv + tile * BLOCK, BLOCK), BLOCK)
            for s in range(STEPS)
        ]
        new_key = jnp.concatenate([new_keys[at, :] for at in fresh_at], axis=0)
        new_value = jnp.concatenate([new_values[at, :] for at in fresh_at], axis=0)
        transposed = (((1,), (1,)), ((), ()))
        fresh = lax.dot_general(query, new_key, transposed, preferred_element_type=f32)
        fresh = jnp.where(fresh_live, fresh, -1e30)
        scores = []
        for i in range(near):
            r = tile * near + i
            key = jnp.concatenate([keys[pages[p, r]] for p in range(per_row)], axis=0)
            part = lax.dot_general(
                query[i * mine : (i + 1) * mine], key, transposed, preferred_element_type=f32
            )
            scores.append(jnp.where(old_key < lengths[r] * kv, part, -1e30))
        scores = jnp.concatenate(scores, axis=0)
        top = jnp.maximum(
            jnp.max(scores, axis=-1, keepdims=True), jnp.max(fresh, axis=-1, keepdims=True)
        )
        e_old = jnp.exp2((scores - top) * scale)
        e_new = jnp.exp2((fresh - top) * scale)
        total = jnp.sum(e_old, axis=-1, keepdims=True) + jnp.sum(e_new, axis=-1, keepdims=True)
        share = 1.0 / total
        w_old = (e_old * share).astype(bf16)
        w_new = (e_new * share).astype(bf16)
        result = jnp.dot(w_new, new_value, preferred_element_type=f32)
        for i in range(near):
            r = tile * near + i
            value = jnp.concatenate([values[pages[p, r]] for p in range(per_row)], axis=0)
            both = result[i * mine : (i + 1) * mine] + jnp.dot(
                w_old[i * mine : (i + 1) * mine], value, preferred_element_type=f32
            )
            for s in range(STEPS):
                at = pl.multiple_of((s * rows + r) * BLOCK, BLOCK)
                out_blocks[pl.ds(at, BLOCK), :] = both[s * heads : (s + 1) * heads]
        return 0

    lax.fori_loop(0, rows // near, eight_rows, 0)

    for s in range(STEPS):
        for c in range(BLOCK):
            out_ref[s, :, c * LANES : (c + 1) * LANES] = out_blocks[
                pl.ds(s * rows * BLOCK + c, rows, stride=BLOCK), :
            ].astype(bf16)


def every_slot_kernel(
    rows,
    ctx,
    page,
    slot_row,
    row_answer,
    pages,
    lengths,
    picks,
    x_hbm,
    base_hbm,
    down_hbm,
    up_hbm,
    key_hbm,
    value_hbm,
    new_key_hbm,
    new_value_hbm,
    out_ref,
    x_in,
    base_in,
    down,
    up,
    keys,
    values,
    new_keys,
    new_values,
    x_blocks,
    base_blocks,
    out_blocks,
    sent,
    got,
    got_picks,
    masks,
    own_part,
    parts,
    wide,
    answers,
    returned,
    local_sems,
    x_send,
    x_recv,
    pick_send,
    pick_recv,
    part_send,
    part_recv,
    answer_send,
    answer_recv,
):
    me = lax.axis_index("pool")
    my_tp = lax.axis_index("tp")
    f32, bf16 = jnp.float32, jnp.bfloat16

    barrier = greet_all(me, my_tp)
    loads = start_loads(
        (
            (x_hbm, x_in),
            (down_hbm, down),
            (up_hbm, up),
            (base_hbm, base_in),
            (key_hbm, keys),
            (value_hbm, values),
            (new_key_hbm, new_keys),
            (new_value_hbm, new_values),
        ),
        local_sems,
    )
    loads[0].wait()
    to_blocks(rows, x_in, base_blocks)
    x_blocks[...] = base_blocks[...].astype(bf16).reshape(STEPS * rows, BLOCK, LANES)

    pl.semaphore_wait(barrier, POOL - 1 + TP - 1)

    def message(k, src, dst, send_sem, recv_sem, to):
        return pltpu.make_async_remote_copy(
            src_ref=src.at[pl.ds(k * PER, PER)],
            dst_ref=dst.at[pl.ds(k * PER, PER)],
            send_sem=send_sem,
            recv_sem=recv_sem,
            device_id={"pool": to},
            device_id_type=MESH,
        )

    def blocks_of(k, dst):
        for j in range(SLOTS):
            row = slot_row[k * SLOTS + j]
            for s in range(STEPS):
                dst[k * PER + s * SLOTS + j] = x_blocks[row + s * rows]

    def send_row(k, _):
        blocks_of(k, sent)
        to = ahead(me, k)
        pltpu.make_async_remote_copy(
            src_ref=picks.at[k],
            dst_ref=got_picks.at[k],
            send_sem=pick_send,
            recv_sem=pick_recv.at[k // GROUP],
            device_id={"pool": to},
            device_id_type=MESH,
        ).start()
        message(k, sent, got, x_send, x_recv.at[k // GROUP], to).start()
        return 0

    lax.fori_loop(1, POOL, send_row, 0)
    blocks_of(0, got)
    got_picks[0] = picks[0]

    loads[1].wait()
    loads[2].wait()

    grows = GROUP * PER
    width = down.shape[0]
    rank = width // 8
    spread = (
        lax.broadcasted_iota(jnp.int32, (grows, GROUP), 0) // PER
        == lax.broadcasted_iota(jnp.int32, (grows, GROUP), 1)
    ).astype(f32)
    lane = lax.broadcasted_iota(jnp.int32, (grows, LANES), 1)
    slot = lax.broadcasted_iota(jnp.int32, (grows, LANES), 0) % SLOTS
    slot_lanes = (lane // 8 == slot).astype(f32)
    widen = (
        lax.broadcasted_iota(jnp.int32, (LANES, width), 0) % 8
        == lax.broadcasted_iota(jnp.int32, (LANES, width), 1) // rank
    ).astype(f32)

    def group_bytes(g, first, ref, per, sem):
        lo, n = g * GROUP * per, GROUP * per
        if first:
            lo, n = per, (GROUP - 1) * per
        part = ref.at[pl.ds(lo, n)]
        pltpu.make_async_copy(part, part, sem).wait()

    def project_down(g, first):
        group_bytes(g, first, got, PER, x_recv.at[g])
        group_bytes(g, first, got_picks, 1, pick_recv.at[g])
        wide[...] = got[pl.ds(g * grows, grows)].reshape(grows * BLOCK, LANES).astype(f32)
        features = jnp.concatenate(
            [wide[pl.ds(c, grows, stride=BLOCK), :] for c in range(BLOCK)], axis=1
        ).astype(bf16)
        product = lax.dot_general(
            features, down[...], (((1,), (1,)), ((), ())), preferred_element_type=f32
        )
        chosen = got_picks[pl.ds(g * GROUP, GROUP)].reshape(GROUP, LANES)
        chosen = jnp.dot(spread, chosen, preferred_element_type=f32) * slot_lanes
        mask = jnp.dot(chosen, widen, preferred_element_type=f32)
        masks[g] = mask.astype(bf16)
        product = product * mask
        part = product[:, :LANES]
        for i in range(1, width // LANES):
            part = part + product[:, i * LANES : (i + 1) * LANES]
        own_part[g] = part
        for t in range(1, TP):
            pltpu.make_async_remote_copy(
                src_ref=own_part.at[g],
                dst_ref=parts.at[g, t - 1],
                send_sem=part_send,
                recv_sem=part_recv.at[g],
                device_id={"tp": (my_tp + t) % TP},
                device_id_type=MESH,
            ).start()

    def project_up(g, first):
        pltpu.make_async_copy(parts.at[g], parts.at[g], part_recv.at[g]).wait()
        u = own_part[g] + parts[g, 0] + parts[g, 1] + parts[g, 2]
        u = u.astype(bf16)
        u = jnp.concatenate([u] * (width // LANES), axis=1) * masks[g]
        delta = jnp.dot(u, up[...], preferred_element_type=f32) * ADAPTER_SCALE
        for c in range(BLOCK):
            wide[pl.ds(c, grows, stride=BLOCK), :] = delta[:, c * LANES : (c + 1) * LANES]
        answers[pl.ds(g * grows, grows)] = (
            wide[...].astype(bf16).reshape(grows, BLOCK, LANES)
        )

        def answer(k, _):
            message(k, answers, returned, answer_send, answer_recv, behind(me, k)).start()
            return 0

        if first:
            returned[pl.ds(0, PER)] = answers[pl.ds(0, PER)]
            lax.fori_loop(1, GROUP, answer, 0)
        else:
            lax.fori_loop(g * GROUP, (g + 1) * GROUP, answer, 0)

    project_down(0, True)
    project_down(1, False)
    project_up(0, True)

    def advance(g, _):
        project_down(g, False)
        project_up(g - 1, False)
        return 0

    lax.fori_loop(2, GROUPS, advance, 0)
    project_up(GROUPS - 1, False)

    for load in loads[3:]:
        load.wait()
    to_blocks(rows, base_in, base_blocks)

    tail = returned.at[pl.ds(PER, (POOL - 1) * PER)]
    pltpu.make_async_copy(tail, tail, answer_recv).wait()

    attend(
        rows,
        ctx,
        page,
        row_answer,
        pages,
        lengths,
        keys,
        values,
        new_keys,
        new_values,
        base_blocks,
        returned,
        out_blocks,
        out_ref,
    )

    others = sent.at[pl.ds(PER, (POOL - 1) * PER)]
    pltpu.make_async_copy(others, others, x_send).wait()
    others = answers.at[pl.ds(PER, (POOL - 1) * PER)]
    pltpu.make_async_copy(others, others, answer_send).wait()
    others = got_picks.at[pl.ds(1, POOL - 1)]
    pltpu.make_async_copy(others, others, pick_send).wait()
    pltpu.make_async_copy(parts, parts, part_send).wait()


def shared_chip_kernel(
    rows,
    ctx,
    page,
    slot_row,
    third_row,
    row_answer,
    pages,
    lengths,
    picks,
    x_hbm,
    base_hbm,
    down_hbm,
    up_hbm,
    key_hbm,
    value_hbm,
    new_key_hbm,
    new_value_hbm,
    out_ref,
    full_ref,
    x_in,
    base_in,
    down,
    up,
    keys,
    values,
    new_keys,
    new_values,
    x_blocks,
    base_blocks,
    out_blocks,
    sent,
    got,
    got_picks,
    masks,
    own_part,
    parts,
    wide,
    answers,
    returned,
    local_sems,
    weight_send,
    weight_recv,
    x_send,
    x_recv,
    pick_send,
    pick_recv,
    part_send,
    part_recv,
    answer_send,
    answer_recv,
):
    me = lax.axis_index("pool")
    my_tp = lax.axis_index("tp")
    my_core = me % C
    f32, bf16 = jnp.float32, jnp.bfloat16
    three = THREE

    barrier = greet_all(me, my_tp)
    width = down_hbm.shape[0]
    my_part = pl.ds(pl.multiple_of(my_core * width, width), width)
    loads = start_loads(
        (
            (x_hbm, x_in),
            (down_hbm, down.at[my_part]),
            (up_hbm, up.at[my_part]),
            (base_hbm, base_in),
            (key_hbm, keys),
            (value_hbm, values),
            (new_key_hbm, new_keys),
            (new_value_hbm, new_values),
        ),
        local_sems,
    )
    loads[0].wait()
    to_blocks(rows, x_in, base_blocks)
    x_blocks[...] = base_blocks[...].astype(bf16).reshape(STEPS * rows, BLOCK, LANES)

    pl.semaphore_wait(barrier, POOL - 1 + TP - 1)

    def push(src, dst, send_sem, recv_sem, to):
        pltpu.make_async_remote_copy(
            src_ref=src,
            dst_ref=dst,
            send_sem=send_sem,
            recv_sem=recv_sem,
            device_id={"pool": to},
            device_id_type=MESH,
        ).start()

    def message(ref, k, n):
        return ref.at[pl.ds(k * n, n)]

    def blocks_of(k, dst):
        row = slot_row[k]
        for s in range(STEPS):
            dst[k * three + s] = x_blocks[row + s * rows]
        dst[k * three + STEPS] = x_blocks[third_row[k] + (ahead(me, k) % C) * rows]

    def send_row(k, _):
        blocks_of(k, sent)
        to, b = ahead(me, k), k // BATCH
        push(message(picks, k, 1), message(got_picks, k, 1), pick_send, pick_recv.at[b], to)
        push(message(sent, k, three), message(got, k, three), x_send, x_recv.at[b], to)
        return 0

    lax.fori_loop(1, BATCH, send_row, 0)
    other = ahead(me, Z)
    push(down_hbm, down.at[my_part], weight_send.at[0], weight_recv.at[0], other)
    lax.fori_loop(BATCH, 2 * BATCH, send_row, 0)
    push(up_hbm, up.at[my_part], weight_send.at[1], weight_recv.at[1], other)
    lax.fori_loop(2 * BATCH, POOL, send_row, 0)
    blocks_of(0, got)
    got_picks[0] = picks[0]

    loads[3].wait()
    to_blocks(rows, base_in, base_blocks)

    held = 8
    rank = width // held
    both = C * held
    brows = BATCH * three
    spread = (
        lax.broadcasted_iota(jnp.int32, (brows, BATCH), 0) // three
        == lax.broadcasted_iota(jnp.int32, (brows, BATCH), 1)
    ).astype(f32)
    slot_lanes = (
        lax.broadcasted_iota(jnp.int32, (brows, LANES), 1) // both
        == (lax.broadcasted_iota(jnp.int32, (brows, LANES), 0) % three) // STEPS
    ).astype(f32)
    widen = (
        lax.broadcasted_iota(jnp.int32, (LANES, C * width), 0) % both
        == lax.broadcasted_iota(jnp.int32, (LANES, C * width), 1) // rank
    ).astype(f32)

    def down_batch(b):
        first = 1 if b == 0 else 0
        await_bytes(got_picks.at[pl.ds(b * BATCH + first, BATCH - first)], pick_recv.at[b])
        chosen = got_picks[pl.ds(b * BATCH, BATCH)].reshape(BATCH, LANES)
        chosen = jnp.dot(spread, chosen, preferred_element_type=f32) * slot_lanes
        mask = jnp.dot(chosen, widen, preferred_element_type=f32)
        masks[b] = mask.astype(bf16)
        await_bytes(
            got.at[pl.ds(b * brows + first * three, brows - first * three)], x_recv.at[b]
        )
        blocks = got[pl.ds(b * brows, brows)]
        wide[...] = blocks.reshape(brows * BLOCK, LANES).astype(f32)
        features = jnp.concatenate(
            [wide[pl.ds(c, brows, stride=BLOCK), :] for c in range(BLOCK)], axis=1
        ).astype(bf16)
        product = lax.dot_general(
            features, down[...], (((1,), (1,)), ((), ())), preferred_element_type=f32
        )
        product = product * mask
        part = product[:, :LANES]
        for i in range(1, C * width // LANES):
            part = part + product[:, i * LANES : (i + 1) * LANES]
        own_part[b] = part
        for t in range(1, TP):
            pltpu.make_async_remote_copy(
                src_ref=own_part.at[b],
                dst_ref=parts.at[b, t - 1],
                send_sem=part_send,
                recv_sem=part_recv.at[b],
                device_id={"tp": (my_tp + t) % TP},
                device_id_type=MESH,
            ).start()

    def up_batch(b):
        await_bytes(parts.at[b], part_recv.at[b])
        u = own_part[b] + parts[b, 0] + parts[b, 1] + parts[b, 2]
        u = jnp.concatenate([u.astype(bf16)] * (C * width // LANES), axis=1) * masks[b]
        delta = jnp.dot(u, up[...], preferred_element_type=f32) * ADAPTER_SCALE
        for c in range(BLOCK):
            wide[pl.ds(c, brows, stride=BLOCK), :] = delta[:, c * LANES : (c + 1) * LANES]
        answers[pl.ds(b * brows, brows)] = wide[...].astype(bf16).reshape(brows, BLOCK, LANES)

        def answer(k, _):
            push(
                message(answers, k, three),
                message(returned, k, three),
                answer_send,
                answer_recv,
                behind(me, k),
            )
            return 0

        if b == 0:
            returned[pl.ds(0, three)] = answers[pl.ds(0, three)]
        lax.fori_loop(max(b * BATCH, 1), (b + 1) * BATCH, answer, 0)

    loads[1].wait()
    await_bytes(down.at[my_part], weight_recv.at[0])
    down_batch(0)
    down_batch(1)
    loads[2].wait()
    await_bytes(up.at[my_part], weight_recv.at[1])
    up_batch(0)
    for b in range(2, BATCHES):
        down_batch(b)
        up_batch(b - 1)
    up_batch(BATCHES - 1)

    full_ref[0, 0] = jnp.max(got_picks[...].reshape(POOL, LANES)[:, 2 * both]).astype(jnp.int32)
    for load in loads[4:]:
        load.wait()
    await_bytes(returned.at[pl.ds(three, (POOL - 1) * three)], answer_recv)
    attend(
        rows,
        ctx,
        page,
        row_answer,
        pages,
        lengths,
        keys,
        values,
        new_keys,
        new_values,
        base_blocks,
        returned,
        out_blocks,
        out_ref,
    )

    await_bytes(down.at[my_part], weight_send.at[0])
    await_bytes(up.at[my_part], weight_send.at[1])
    await_bytes(sent.at[pl.ds(three, (POOL - 1) * three)], x_send)
    await_bytes(got_picks.at[pl.ds(1, POOL - 1)], pick_send)
    await_bytes(parts, part_send)
    await_bytes(answers.at[pl.ds(three, (POOL - 1) * three)], answer_send)


def compiler_params(collective_id):
    return pltpu.CompilerParams(
        collective_id=collective_id, has_side_effects=True, vmem_limit_bytes=60 << 20
    )


def shards(
    normed_input,
    base_query_output,
    adapter_down_weight,
    adapter_up_weight,
    row_adapter_index,
    paged_key_cache,
    paged_value_cache,
    step_token_keys,
    step_token_values,
    row_page_table,
    lengths,
):
    rows = row_adapter_index.shape[0]
    features = normed_input.shape[2]
    held, rank = adapter_up_weight.shape[:2]
    count, page, kv, head = paged_key_cache.shape
    ctx = page * row_page_table.shape[1]
    width = held * rank
    me = lax.axis_index("pool")
    bf16, f32 = jnp.bfloat16, jnp.float32
    smem = pl.BlockSpec(memory_space=pltpu.SMEM)
    vmem = pl.BlockSpec(memory_space=pltpu.VMEM)
    anywhere = pl.BlockSpec(memory_space=pl.ANY)
    dma = pltpu.SemaphoreType.DMA

    order = jnp.arange(rows, dtype=jnp.int32)
    positions = jnp.arange(POOL, dtype=jnp.int32)
    lane = jnp.arange(LANES, dtype=jnp.int32)

    def among(same):
        return jnp.sum((same & (order[None, :] < order[:, None])).astype(jnp.int32), axis=1)

    arrays = (
        normed_input,
        base_query_output,
        adapter_down_weight.transpose(1, 2, 0).reshape(width, features),
        adapter_up_weight.reshape(width, features),
        paged_key_cache.reshape(count, page * kv, head),
        paged_value_cache.reshape(count, page * kv, head),
        step_token_keys.reshape(STEPS * rows * kv, head),
        step_token_values.reshape(STEPS * rows * kv, head),
    )
    staged = [
        pltpu.VMEM((STEPS, rows, features), bf16),
        pltpu.VMEM((STEPS, rows, features), bf16),
    ]
    staged_rest = [
        pltpu.VMEM((count, page * kv, head), bf16),
        pltpu.VMEM((count, page * kv, head), bf16),
        pltpu.VMEM((STEPS * rows * kv, head), bf16),
        pltpu.VMEM((STEPS * rows * kv, head), bf16),
        pltpu.VMEM((STEPS * rows, BLOCK, LANES), bf16),
        pltpu.VMEM((STEPS * rows * BLOCK, LANES), f32),
        pltpu.VMEM((STEPS * rows * BLOCK, LANES), f32),
    ]
    result = jax.ShapeDtypeStruct((STEPS, rows, features), bf16)
    cost = pl.CostEstimate(
        flops=3_000_000_000, bytes_accessed=12_000_000, transcendentals=1_000_000
    )

    def blocks(n):
        return pltpu.VMEM((n, BLOCK, LANES), bf16)

    def weights(n):
        return [pltpu.VMEM((n * width, features), bf16)] * 2

    def shared_chip():
        chip = row_adapter_index // (C * held)
        rank_there = among(chip[None, :] == chip[:, None])
        core_of = jnp.arange(C, dtype=jnp.int32)
        there = position(me, chip[:, None] * C + core_of[None, :])
        whole = jnp.sum(jnp.where(rank_there[:, None] == core_of[None, :], there, 0), axis=1)
        whole = jnp.where(rank_there < C, whole, -1)
        to_whole = positions[:, None] == whole[None, :]
        third = rank_there == C
        to_third = jnp.any(positions[:, None, None] == there[None, :, :], axis=2) & third[None, :]
        slot_row = jnp.sum(jnp.where(to_whole, order[None, :], 0), axis=1)
        third_row = jnp.sum(jnp.where(to_third, order[None, :], 0), axis=1)
        row_answer = jnp.where(
            rank_there[None, :] < C,
            jnp.maximum(whole, 0)[None, :] * THREE + core_of[:, None],
            there.T * THREE + STEPS,
        )
        named = row_adapter_index % (C * held)
        picks = sum(
            jnp.dot(
                aimed.astype(bf16),
                (named[:, None] + i * C * held == lane[None, :]).astype(bf16),
                preferred_element_type=f32,
            )
            for i, aimed in enumerate((to_whole, to_third))
        )
        full = jnp.any(rank_there > C).astype(f32)
        picks = jnp.where(lane[None, :] == 2 * C * held, full, picks)
        n = POOL * THREE
        brows = BATCH * THREE
        return pl.pallas_call(
            functools.partial(shared_chip_kernel, rows, ctx, page),
            out_shape=(result, jax.ShapeDtypeStruct((1, 1), jnp.int32)),
            in_specs=[smem] * 5 + [vmem] + [anywhere] * 8,
            out_specs=(vmem, smem),
            scratch_shapes=staged
            + weights(C)
            + staged_rest
            + [
                blocks(n),
                blocks(n),
                pltpu.VMEM((POOL, 1, LANES), f32),
                pltpu.VMEM((BATCHES, brows, C * width), bf16),
                pltpu.VMEM((BATCHES, brows, LANES), f32),
                pltpu.VMEM((BATCHES, TP - 1, brows, LANES), f32),
                pltpu.VMEM((brows * BLOCK, LANES), f32),
                blocks(n),
                blocks(n),
                dma((8,)),
                dma((2,)),
                dma((2,)),
                dma,
                dma((BATCHES,)),
                dma,
                dma((BATCHES,)),
                dma,
                dma((BATCHES,)),
                dma,
                dma,
            ],
            compiler_params=compiler_params(0),
            cost_estimate=cost,
            name="shared_chip_and_attention",
        )(
            slot_row,
            third_row,
            row_answer,
            row_page_table.T,
            lengths,
            picks.reshape(POOL, 1, LANES),
            *arrays,
        )

    def every_slot():
        owner = row_adapter_index // held
        earlier = among(owner[None, :] == owner[:, None])
        toward = position(me, owner)
        wanted = earlier[:, None] * held + row_adapter_index[:, None] % held == lane[None, :]
        aimed = positions[:, None] == toward[None, :]
        picks = jnp.dot(aimed.astype(bf16), wanted.astype(bf16), preferred_element_type=f32)
        row_slot = toward * SLOTS + earlier
        place = jnp.arange(POOL * SLOTS, dtype=jnp.int32)[:, None] == row_slot[None, :]
        slot_row = jnp.sum(jnp.where(place, order[None, :], 0), axis=1)
        n = POOL * PER
        grows = GROUP * PER
        return pl.pallas_call(
            functools.partial(every_slot_kernel, rows, ctx, page),
            out_shape=result,
            in_specs=[smem] * 4 + [vmem] + [anywhere] * 8,
            out_specs=vmem,
            scratch_shapes=staged
            + weights(1)
            + staged_rest
            + [
                blocks(n),
                blocks(n),
                pltpu.VMEM((POOL, 1, LANES), f32),
                pltpu.VMEM((GROUPS, grows, width), bf16),
                pltpu.VMEM((GROUPS, grows, LANES), f32),
                pltpu.VMEM((GROUPS, TP - 1, grows, LANES), f32),
                pltpu.VMEM((grows * BLOCK, LANES), f32),
                blocks(n),
                blocks(n),
                dma((8,)),
                dma,
                dma((GROUPS,)),
                dma,
                dma((GROUPS,)),
                dma,
                dma((GROUPS,)),
                dma,
                dma,
            ],
            compiler_params=compiler_params(1),
            cost_estimate=cost,
            name="every_slot_and_attention",
        )(
            slot_row,
            toward[None, :] * PER + earlier[None, :] + SLOTS * jnp.arange(STEPS)[:, None],
            row_page_table.T,
            lengths,
            picks.reshape(POOL, 1, LANES),
            *arrays,
        )

    attended, full = shared_chip()
    return lax.cond(full[0, 0] > 0, every_slot, lambda: attended)


def solution(mesh):
    placed = (
        P(None, "pool", "tp"),
        P(None, "pool", "tp"),
        P("tp", "pool", None),
        P("pool", None, "tp"),
        P("pool"),
        P("pool", None, "tp", None),
        P("pool", None, "tp", None),
        P(None, "pool", "tp", None),
        P(None, "pool", "tp", None),
        P("pool", None),
        P("pool"),
    )
    return jax.shard_map(
        shards, mesh=mesh, in_specs=placed, out_specs=P(None, "pool", "tp"), check_vma=False
    )
```

time: 86.3 us -> 63.9 us (0.74)
  Pallas kernels: 78.8 us -> 56.4 us
  local copies, waits for them, and re-layouts: 3.21 us -> 1.88 us
  between operations: 0.02 us -> 1.3 us
  other arithmetic: 4.08 us -> 2.89 us
  matrix products: 0 us -> 1.15 us
    pallas_call x1, Pallas kernels: 78.8 us -> 56.4 us  [shared_chip(): pl.pallas_call(functools.partial(shared_chip_kernel, rows, ctx, page), ou...]
    unnamed x2 -> x11, local copies, waits for them, and re-layouts: 2.53 us -> 0.77 us
    reduce_sum x3, other arithmetic: 2.03 us -> 0.86 us  [the longest x1 0.64 us: shared_chip(): third_row = jnp.sum(jnp.where(to_third, order[None, :], 0), axis=1)]
    dot_general x0 -> x2, matrix products: none -> 1.15 us  [shared_chip(): jnp.dot(aimed.astype(bf16), (named[:, None] + i * C * held == lane[None,...]
    iota x0 -> x3, local copies, waits for them, and re-layouts: none -> 1.11 us  [the longest x1 0.57 us: shards(): lane = jnp.arange(LANES, dtype=jnp.int32)]
where the time goes in v3:
time: 63.9 us; the launch traced here: 63.8 us
  Pallas kernels  56.4 us (88%)
  other arithmetic  2.89 us (5%)
  local copies, waits for them, and re-layouts  1.88 us (3%)
  between operations  1.3 us (2%)
  matrix products  1.15 us (2%)
    pallas_call x1, Pallas kernels, shared_chip(): pl.pallas_call(functools.partial(shared_chip_kernel, rows, ctx, page), ou...  56.4 us

profile of v3, /device:TPU:1, one launch (start us, length us, event | category | flops | bytes accessed | tf_op | source)
XLA Modules:
  0.0 63.8 jit_solution(760450605153067922)
XLA Ops:
  0.0 0.6 iota.55
  0.6 0.5 iota.54
  1.1 0.7 %broadcast_add_fusion.1 = (s32[48]{0:T(128)S(1)}, s32[48]{0:T(128)S(1)}, s32[48]{0:T(128)S(1)}, s32[48]{0:T(128)S(1)}) fusion(s32[48]{0:T(128)} %param.17), kind=kLoop, calls=%fused_computation.144 | loop fusion | flops 1008 | bytes 960 | tf_op jit(solution)/shard_map/add | solution.py:733
  1.8 0.2 convert_reduce_fusion.1
  2.0 0.6 %compare_reduce_fusion = (pred[]{:T(512)}, pred[48]{0:T(512)(128)(4,1)S(1)}, pred[48]{0:T(512)(128)(4,1)S(1)}) fusion(s32[48]{0:T(128)S(1)} %convert_reduce_fusion.1), kind=kLoop, calls=%fused_computation.86 | loop fusion | flops 191 | bytes 289 | tf_op jit(solution)/shard_map/reduce_or | solution.py:738
  3.3 0.6 add_select_fusion.row_answer
  3.9 0.1 fusion.20
  4.0 0.6 select_reduce_fusion.1
  4.7 0.3 fusion.21
  4.9 0.9 %fusion.19 = f32[64,128]{1,0:T(8,128)} fusion(f32[64,128]{1,0:T(8,128)S(1)} %fusion.21, pred[64,48]{0,1:T(8,128)(4,1)S(1)} %fusion.20, f32[]{:T(128)S(6)} %convert_element_type.22, pred[128]{0:T(512)(128)(4,1)S(1)} %iota_compare_fusion.9, s32[48]{0:T(128)S(1)} %get-tuple-element.63, pred[48]{0:T(512)(128)(4,1)S(1)} %get-tuple-element.73), kind=kOutput, calls=%fused_computation.52 | convolution fusion | flops 812032 | bytes 68980 | tf_op jit(solution)/shard_map/dot_general | solution.py:731
  5.8 0.0 copy-start
  5.8 0.0 copy-start.1
  5.8 0.0 copy-start.2
  5.8 0.0 copy-start.3
  5.8 0.0 copy-start.4
  5.8 56.4 %shared_chip_and_attention.1 = (bf16[2,48,2048]{2,1,0:T(8,128)(2,1)S(1)}, s32[1,1]{1,0:T(1,128)}) custom-call(s32[64]{0:T(128)} %get-tuple-element.78.slot_row, s32[64]{0:T(128)} %get-tuple-element.77.third_row, s32[2,48]{1,0:T(2,128)} %add_select_fusion.row_answer, s32[4,48]{1,0:T(4,128)} %bitcast.27, s32[48]{0:T(128)} %lengths.1, f32[64,1,128]{2,1,0:T(1,128)} %bitcast.25, ...), custom_call_target="tpu_custom_call" | custom-call | flops 3000000000 | bytes 12000000 | tf_op jit(solution)/shard_map/shared_chip_and_attention/pallas_call | solution.py:742
  62.8 0.0 copy-done
  62.8 0.0 copy-done.1
  62.8 0.0 copy-done.2
  62.8 0.0 copy-done.3
  62.8 0.0 copy-done.4
  62.8 0.2 conditional.1
  63.0 0.7 %copy.17 = bf16[2,48,2048]{2,1,0:T(8,128)(2,1)} copy(bf16[2,48,2048]{2,1,0:T(8,128)(2,1)S(1)} %get-tuple-element.60) | data formatting | bytes 786432
  (4 shorter events, 0.1 us)
Async XLA Ops:
  5.8 57.0 %copy-start = (bf16[192,32,2,128]{3,2,1,0:T(2,128)(2,1)S(1)}, bf16[192,32,2,128]{3,2,1,0:T(2,128)(2,1)}, u32[]{:S(2)}) copy-start(bf16[192,32,2,128]{3,2,1,0:T(2,128)(2,1)} %param.18) | copy-start | bytes 9437188
  5.8 57.0 %copy-start.1 = (bf16[2,48,2048]{2,1,0:T(8,128)(2,1)S(1)}, bf16[2,48,2048]{2,1,0:T(8,128)(2,1)}, u32[]{:S(2)}) copy-start(bf16[2,48,2048]{2,1,0:T(8,128)(2,1)} %x_hbm.1) | copy-start | bytes 1179652
  5.8 57.0 %copy-start.2 = (s32[48,4]{0,1:T(4,128)S(1)}, s32[48,4]{0,1:T(4,128)}, u32[]{:S(2)}) copy-start(s32[48,4]{0,1:T(4,128)} %param.22) | copy-start | bytes 2308
  5.8 57.0 %copy-start.3 = (s32[48]{0:T(128)S(1)}, s32[48]{0:T(128)}, u32[]{:S(2)}) copy-start(s32[48]{0:T(128)} %lengths.1) | copy-start | bytes 580
  5.8 57.0 %copy-start.4 = (s32[48]{0:T(128)S(1)}, s32[48]{0:T(128)}, u32[]{:S(2)}) copy-start(s32[48]{0:T(128)} %param.17) | copy-start | bytes 580

commit v4 on v3

--- a/solution.py
+++ b/solution.py
@@ -145,7 +145,7 @@
             part = lax.dot_general(
                 query[i * mine : (i + 1) * mine], key, transposed, preferred_element_type=f32
             )
-            scores.append(jnp.where(old_key < lengths[r] * kv, part, -1e30))
+            scores.append(jnp.where(old_key < lengths[0, r] * kv, part, -1e30))
         scores = jnp.concatenate(scores, axis=0)
         top = jnp.maximum(
             jnp.max(scores, axis=-1, keepdims=True), jnp.max(fresh, axis=-1, keepdims=True)
@@ -168,7 +168,7 @@
                 out_blocks[pl.ds(at, BLOCK), :] = both[s * heads : (s + 1) * heads]
         return 0
 
-    lax.fori_loop(0, rows // near, eight_rows, 0)
+    lax.fori_loop(0, rows // near, eight_rows, 0, unroll=2)
 
     for s in range(STEPS):
         for c in range(BLOCK):
@@ -408,12 +408,9 @@
     rows,
     ctx,
     page,
-    slot_row,
-    third_row,
-    row_answer,
-    pages,
-    lengths,
-    picks,
+    adapter_hbm,
+    pages_hbm,
+    lengths_hbm,
     x_hbm,
     base_hbm,
     down_hbm,
@@ -424,6 +421,12 @@
     new_value_hbm,
     out_ref,
     full_ref,
+    adapters,
+    answer_table,
+    row_answer,
+    pages,
+    lengths,
+    picks,
     x_in,
     base_in,
     down,
@@ -432,7 +435,6 @@
     values,
     new_keys,
     new_values,
-    x_blocks,
     base_blocks,
     out_blocks,
     sent,
@@ -445,6 +447,7 @@
     answers,
     returned,
     local_sems,
+    table_sem,
     weight_send,
     weight_recv,
     x_send,
@@ -462,11 +465,11 @@
     f32, bf16 = jnp.float32, jnp.bfloat16
     three = THREE
 
-    barrier = greet_all(me, my_tp)
     width = down_hbm.shape[0]
     my_part = pl.ds(pl.multiple_of(my_core * width, width), width)
     loads = start_loads(
         (
+            (adapter_hbm, adapters),
             (x_hbm, x_in),
             (down_hbm, down.at[my_part]),
             (up_hbm, up.at[my_part]),
@@ -475,13 +478,77 @@
             (value_hbm, values),
             (new_key_hbm, new_keys),
             (new_value_hbm, new_values),
+            (pages_hbm, pages),
+            (lengths_hbm, lengths),
         ),
         local_sems,
     )
+    barrier = greet_all(me, my_tp)
+
+    held = 8
+    both = C * held
+    rank = width // held
     loads[0].wait()
-    to_blocks(rows, x_in, base_blocks)
-    x_blocks[...] = base_blocks[...].astype(bf16).reshape(STEPS * rows, BLOCK, LANES)
-
+    i32 = jnp.int32
+
+    def iota(shape, axis):
+        return lax.broadcasted_iota(i32, shape, axis)
+
+    square = (rows, rows)
+    across = adapters[...]
+    down_wards = jnp.sum(
+        jnp.where(iota(square, 0) == iota(square, 1), across.astype(f32), 0.0), axis=1, keepdims=True
+    ).astype(i32)
+    same_chip = across // both == down_wards // both
+    order = jnp.sum(
+        (same_chip & (iota(square, 0) < iota(square, 1))).astype(f32), axis=0, keepdims=True
+    ).astype(i32)
+    chip = across // both
+    dy = (chip // Z + Y - me // (Z * C)) % Y
+    dz = (chip % Z + Z - (me // C) % Z) % Z
+    chip_at = dy * (Z * C) + dz
+    whole = jnp.where(order < C, chip_at + (order + C - my_core) % C * Z, -1)
+    third = jnp.where(order == C, chip_at, -1)
+    full = jnp.max((order > C).astype(f32), axis=1, keepdims=True)
+    for s in range(STEPS):
+        split = (chip_at + (s + C - my_core) % C * Z) * three + STEPS
+        answer_table[s : s + 1, :rows] = jnp.where(order < C, whole * three + s, split)
+    table = pltpu.make_async_copy(answer_table, row_answer, table_sem)
+    table.start()
+
+    spots = (POOL, rows)
+    to_whole = (iota(spots, 0) == whole).astype(f32)
+    to_third = (iota(spots, 0) - (iota(spots, 0) // Z) % C * Z == third).astype(f32)
+    named = down_wards % both
+    lanes = iota((rows, LANES), 1)
+    listed = (
+        jnp.dot(to_whole, (lanes == named).astype(f32), preferred_element_type=f32)
+        + jnp.dot(to_third, (lanes == named + both).astype(f32), preferred_element_type=f32)
+        + jnp.where(iota((POOL, LANES), 1) == 2 * both, full, 0.0)
+    )
+    picks[...] = listed.reshape(POOL, 1, LANES)
+    loads[1].wait()
+
+    brows = BATCH * three
+
+    def build(b, dst):
+        shape = (brows, rows)
+        line = iota(shape, 0)
+        at, part = line // three + b * BATCH, line % three
+        its_core = (my_core + (at // Z) % C) % C
+        its_chip = at - (at // Z) % C * Z
+        total = None
+        for s in range(STEPS):
+            hit = ((at == whole) & (part == s)) | (
+                (its_chip == third) & (part == STEPS) & (its_core == s)
+            )
+            term = jnp.dot(hit.astype(bf16), x_in[s], preferred_element_type=f32)
+            total = term if total is None else total + term
+        for c in range(BLOCK):
+            wide[pl.ds(c, brows, stride=BLOCK), :] = total[:, c * LANES : (c + 1) * LANES]
+        dst[pl.ds(b * brows, brows)] = wide[...].astype(bf16).reshape(brows, BLOCK, LANES)
+
+    build(0, sent)
     pl.semaphore_wait(barrier, POOL - 1 + TP - 1)
 
     def push(src, dst, send_sem, recv_sem, to):
@@ -497,35 +564,26 @@
     def message(ref, k, n):
         return ref.at[pl.ds(k * n, n)]
 
-    def blocks_of(k, dst):
-        row = slot_row[k]
-        for s in range(STEPS):
-            dst[k * three + s] = x_blocks[row + s * rows]
-        dst[k * three + STEPS] = x_blocks[third_row[k] + (ahead(me, k) % C) * rows]
-
     def send_row(k, _):
-        blocks_of(k, sent)
         to, b = ahead(me, k), k // BATCH
         push(message(picks, k, 1), message(got_picks, k, 1), pick_send, pick_recv.at[b], to)
         push(message(sent, k, three), message(got, k, three), x_send, x_recv.at[b], to)
         return 0
 
+    other = ahead(me, Z)
     lax.fori_loop(1, BATCH, send_row, 0)
-    other = ahead(me, Z)
     push(down_hbm, down.at[my_part], weight_send.at[0], weight_recv.at[0], other)
-    lax.fori_loop(BATCH, 2 * BATCH, send_row, 0)
-    push(up_hbm, up.at[my_part], weight_send.at[1], weight_recv.at[1], other)
-    lax.fori_loop(2 * BATCH, POOL, send_row, 0)
-    blocks_of(0, got)
+    for b in range(1, BATCHES):
+        build(b, sent)
+        lax.fori_loop(b * BATCH, (b + 1) * BATCH, send_row, 0)
+        if b == 1:
+            push(up_hbm, up.at[my_part], weight_send.at[1], weight_recv.at[1], other)
+    got[pl.ds(0, three)] = sent[pl.ds(0, three)]
     got_picks[0] = picks[0]
 
-    loads[3].wait()
+    loads[4].wait()
     to_blocks(rows, base_in, base_blocks)
 
-    held = 8
-    rank = width // held
-    both = C * held
-    brows = BATCH * three
     spread = (
         lax.broadcasted_iota(jnp.int32, (brows, BATCH), 0) // three
         == lax.broadcasted_iota(jnp.int32, (brows, BATCH), 1)
@@ -595,11 +653,11 @@
             returned[pl.ds(0, three)] = answers[pl.ds(0, three)]
         lax.fori_loop(max(b * BATCH, 1), (b + 1) * BATCH, answer, 0)
 
-    loads[1].wait()
+    loads[2].wait()
     await_bytes(down.at[my_part], weight_recv.at[0])
     down_batch(0)
     down_batch(1)
-    loads[2].wait()
+    loads[3].wait()
     await_bytes(up.at[my_part], weight_recv.at[1])
     up_batch(0)
     for b in range(2, BATCHES):
@@ -608,7 +666,8 @@
     up_batch(BATCHES - 1)
 
     full_ref[0, 0] = jnp.max(got_picks[...].reshape(POOL, LANES)[:, 2 * both]).astype(jnp.int32)
-    for load in loads[4:]:
+    table.wait()
+    for load in loads[5:]:
         load.wait()
     await_bytes(returned.at[pl.ds(three, (POOL - 1) * three)], answer_recv)
     attend(
@@ -668,13 +727,6 @@
     anywhere = pl.BlockSpec(memory_space=pl.ANY)
     dma = pltpu.SemaphoreType.DMA
 
-    order = jnp.arange(rows, dtype=jnp.int32)
-    positions = jnp.arange(POOL, dtype=jnp.int32)
-    lane = jnp.arange(LANES, dtype=jnp.int32)
-
-    def among(same):
-        return jnp.sum((same & (order[None, :] < order[:, None])).astype(jnp.int32), axis=1)
-
     arrays = (
         normed_input,
         base_query_output,
@@ -710,43 +762,25 @@
         return [pltpu.VMEM((n * width, features), bf16)] * 2
 
     def shared_chip():
-        chip = row_adapter_index // (C * held)
-        rank_there = among(chip[None, :] == chip[:, None])
-        core_of = jnp.arange(C, dtype=jnp.int32)
-        there = position(me, chip[:, None] * C + core_of[None, :])
-        whole = jnp.sum(jnp.where(rank_there[:, None] == core_of[None, :], there, 0), axis=1)
-        whole = jnp.where(rank_there < C, whole, -1)
-        to_whole = positions[:, None] == whole[None, :]
-        third = rank_there == C
-        to_third = jnp.any(positions[:, None, None] == there[None, :, :], axis=2) & third[None, :]
-        slot_row = jnp.sum(jnp.where(to_whole, order[None, :], 0), axis=1)
-        third_row = jnp.sum(jnp.where(to_third, order[None, :], 0), axis=1)
-        row_answer = jnp.where(
-            rank_there[None, :] < C,
-            jnp.maximum(whole, 0)[None, :] * THREE + core_of[:, None],
-            there.T * THREE + STEPS,
-        )
-        named = row_adapter_index % (C * held)
-        picks = sum(
-            jnp.dot(
-                aimed.astype(bf16),
-                (named[:, None] + i * C * held == lane[None, :]).astype(bf16),
-                preferred_element_type=f32,
-            )
-            for i, aimed in enumerate((to_whole, to_third))
-        )
-        full = jnp.any(rank_there > C).astype(f32)
-        picks = jnp.where(lane[None, :] == 2 * C * held, full, picks)
         n = POOL * THREE
         brows = BATCH * THREE
         return pl.pallas_call(
             functools.partial(shared_chip_kernel, rows, ctx, page),
             out_shape=(result, jax.ShapeDtypeStruct((1, 1), jnp.int32)),
-            in_specs=[smem] * 5 + [vmem] + [anywhere] * 8,
+            in_specs=[anywhere] * 11,
             out_specs=(vmem, smem),
-            scratch_shapes=staged
+            scratch_shapes=[
+                pltpu.VMEM((1, rows), jnp.int32),
+                pltpu.VMEM((8, LANES), jnp.int32),
+                pltpu.SMEM((8, LANES), jnp.int32),
+                pltpu.SMEM(row_page_table.T.shape, jnp.int32),
+                pltpu.SMEM((1, rows), jnp.int32),
+                pltpu.VMEM((POOL, 1, LANES), f32),
+            ]
+            + staged
             + weights(C)
-            + staged_rest
+            + staged_rest[:4]
+            + staged_rest[5:]
             + [
                 blocks(n),
                 blocks(n),
@@ -757,7 +791,8 @@
                 pltpu.VMEM((brows * BLOCK, LANES), f32),
                 blocks(n),
                 blocks(n),
-                dma((8,)),
+                dma((11,)),
+                dma,
                 dma((2,)),
                 dma((2,)),
                 dma,
@@ -773,18 +808,19 @@
             cost_estimate=cost,
             name="shared_chip_and_attention",
         )(
-            slot_row,
-            third_row,
-            row_answer,
+            row_adapter_index.reshape(1, rows),
             row_page_table.T,
-            lengths,
-            picks.reshape(POOL, 1, LANES),
+            lengths.reshape(1, rows),
             *arrays,
         )
 
     def every_slot():
+        order = jnp.arange(rows, dtype=jnp.int32)
+        positions = jnp.arange(POOL, dtype=jnp.int32)
+        lane = jnp.arange(LANES, dtype=jnp.int32)
         owner = row_adapter_index // held
-        earlier = among(owner[None, :] == owner[:, None])
+        ahead_of = (owner[None, :] == owner[:, None]) & (order[None, :] < order[:, None])
+        earlier = jnp.sum(ahead_of.astype(jnp.int32), axis=1)
         toward = position(me, owner)
         wanted = earlier[:, None] * held + row_adapter_index[:, None] % held == lane[None, :]
         aimed = positions[:, None] == toward[None, :]
@@ -829,7 +865,7 @@
             slot_row,
             toward[None, :] * PER + earlier[None, :] + SLOTS * jnp.arange(STEPS)[:, None],
             row_page_table.T,
-            lengths,
+            lengths.reshape(1, rows),
             picks.reshape(POOL, 1, LANES),
             *arrays,
         )

time: 63.9 us -> 56.7 us (0.89)
  other arithmetic: 2.89 us -> 0 us
  Pallas kernels: 56.4 us -> 55 us
  matrix products: 1.15 us -> 0 us
  local copies, waits for them, and re-layouts: 1.88 us -> 0.77 us
    pallas_call x1, Pallas kernels: 56.4 us -> 55 us  [shared_chip(): pl.pallas_call(functools.partial(shared_chip_kernel, rows, ctx, page), ou...]
    dot_general x2 -> x0, matrix products: 1.15 us -> none  [shared_chip(): jnp.dot(aimed.astype(bf16), (named[:, None] + i * C * held == lane[None,...]
    iota x3 -> x0, local copies, waits for them, and re-layouts: 1.11 us -> none  [the longest x1 0.57 us: shards(): lane = jnp.arange(LANES, dtype=jnp.int32)]
    reduce_sum x3 -> x0, other arithmetic: 0.86 us -> none  [the longest x1 0.64 us: shared_chip(): third_row = jnp.sum(jnp.where(to_third, order[None, :], 0), axis=1)]
    reduce_or x2 -> x0, other arithmetic: 0.72 us -> none  [the longest x1 0.64 us: shared_chip(): full = jnp.any(rank_there > C).astype(f32)]
    add x1 -> x0, other arithmetic: 0.66 us -> none  [shared_chip(): named[:, None] + i * C * held == lane[None, :]]
where the time goes in v4:
time: 56.7 us
  Pallas kernels  55 us (97%)
  local copies, waits for them, and re-layouts  0.77 us (1%)
  between operations  0.69 us (1%)
    pallas_call x1, Pallas kernels, shared_chip(): pl.pallas_call(functools.partial(shared_chip_kernel, rows, ctx, page), ou...  55 us

profile of v4, /device:TPU:1, one launch (start us, length us, event | category | flops | bytes accessed | tf_op | source)
XLA Modules:
  0.0 56.7 jit_solution(6655474388861857941)
XLA Ops:
  0.0 0.0 copy-start
  0.0 0.0 copy-start.1
  0.0 0.0 copy-start.2
  0.0 0.0 copy-start.3
  0.0 0.0 copy-start.4
  0.0 55.0 %shared_chip_and_attention.1 = (bf16[2,48,2048]{2,1,0:T(8,128)(2,1)S(1)}, s32[1,1]{1,0:T(1,128)}) custom-call(s32[1,48]{1,0:T(1,128)} %bitcast.32, s32[4,48]{1,0:T(4,128)} %bitcast.28, s32[1,48]{1,0:T(1,128)} %bitcast.30, bf16[2,48,2048]{2,1,0:T(8,128)(2,1)} %x_hbm.1, bf16[2,48,2048]{2,1,0:T(8,128)(2,1)} %base_hbm.1, bf16[512,2048]{1,0:T(8,128)(2,1)} %bitcast.19, ...), custom_call_target="tpu_custom_call" | custom-call | flops 3000000000 | bytes 12000000 | tf_op jit(solution)/shard_map/shared_chip_and_attention/pallas_call | solution.py:767
  55.7 0.0 copy-done
  55.7 0.0 copy-done.1
  55.7 0.0 copy-done.2
  55.7 0.0 copy-done.3
  55.7 0.0 copy-done.4
  55.7 0.2 conditional.1
  55.9 0.7 %copy.17 = bf16[2,48,2048]{2,1,0:T(8,128)(2,1)} copy(bf16[2,48,2048]{2,1,0:T(8,128)(2,1)S(1)} %get-tuple-element.49) | data formatting | bytes 786432
Async XLA Ops:
  0.0 55.7 %copy-start = (bf16[192,32,2,128]{3,2,1,0:T(2,128)(2,1)S(1)}, bf16[192,32,2,128]{3,2,1,0:T(2,128)(2,1)}, u32[]{:S(2)}) copy-start(bf16[192,32,2,128]{3,2,1,0:T(2,128)(2,1)} %param.18) | copy-start | bytes 9437188
  0.0 55.7 %copy-start.1 = (bf16[2,48,2048]{2,1,0:T(8,128)(2,1)S(1)}, bf16[2,48,2048]{2,1,0:T(8,128)(2,1)}, u32[]{:S(2)}) copy-start(bf16[2,48,2048]{2,1,0:T(8,128)(2,1)} %x_hbm.1) | copy-start | bytes 1179652
  0.0 55.7 %copy-start.2 = (s32[48,4]{0,1:T(4,128)S(1)}, s32[48,4]{0,1:T(4,128)}, u32[]{:S(2)}) copy-start(s32[48,4]{0,1:T(4,128)} %param.22) | copy-start | bytes 2308
  0.0 55.7 %copy-start.3 = (s32[48]{0:T(128)S(1)}, s32[48]{0:T(128)}, u32[]{:S(2)}) copy-start(s32[48]{0:T(128)} %param.23) | copy-start | bytes 580
  0.0 55.7 %copy-start.4 = (s32[48]{0:T(128)S(1)}, s32[48]{0:T(128)}, u32[]{:S(2)}) copy-start(s32[48]{0:T(128)} %param.17) | copy-start | bytes 580

commit v5 on v4

--- a/solution.py
+++ b/solution.py
@@ -168,7 +168,7 @@
                 out_blocks[pl.ds(at, BLOCK), :] = both[s * heads : (s + 1) * heads]
         return 0
 
-    lax.fori_loop(0, rows // near, eight_rows, 0, unroll=2)
+    lax.fori_loop(0, rows // near, eight_rows, 0, unroll=6)
 
     for s in range(STEPS):
         for c in range(BLOCK):

time: 56.7 us -> 56.2 us (level)
  no operation moved by 1% of the time
where the time goes in v5:
time: 56.2 us; the launch traced here: 56.1 us
  Pallas kernels  54.5 us (97%)
  local copies, waits for them, and re-layouts  0.77 us (1%)
  between operations  0.69 us (1%)
    pallas_call x1, Pallas kernels, shared_chip(): pl.pallas_call(functools.partial(shared_chip_kernel, rows, ctx, page), ou...  54.5 us

profile of v5, /device:TPU:1, one launch (start us, length us, event | category | flops | bytes accessed | tf_op | source)
XLA Modules:
  0.0 56.1 jit_solution(699431446345054327)
XLA Ops:
  0.0 0.0 copy-start
  0.0 0.0 copy-start.1
  0.0 0.0 copy-start.2
  0.0 0.0 copy-start.3
  0.0 0.0 copy-start.4
  0.0 54.5 %shared_chip_and_attention.1 = (bf16[2,48,2048]{2,1,0:T(8,128)(2,1)S(1)}, s32[1,1]{1,0:T(1,128)}) custom-call(s32[1,48]{1,0:T(1,128)} %bitcast.32, s32[4,48]{1,0:T(4,128)} %bitcast.28, s32[1,48]{1,0:T(1,128)} %bitcast.30, bf16[2,48,2048]{2,1,0:T(8,128)(2,1)} %x_hbm.1, bf16[2,48,2048]{2,1,0:T(8,128)(2,1)} %base_hbm.1, bf16[512,2048]{1,0:T(8,128)(2,1)} %bitcast.19, ...), custom_call_target="tpu_custom_call" | custom-call | flops 3000000000 | bytes 12000000 | tf_op jit(solution)/shard_map/shared_chip_and_attention/pallas_call | solution.py:767
  55.1 0.0 copy-done
  55.1 0.0 copy-done.1
  55.1 0.0 copy-done.2
  55.1 0.0 copy-done.3
  55.1 0.0 copy-done.4
  55.1 0.2 conditional.1
  55.3 0.7 %copy.17 = bf16[2,48,2048]{2,1,0:T(8,128)(2,1)} copy(bf16[2,48,2048]{2,1,0:T(8,128)(2,1)S(1)} %get-tuple-element.49) | data formatting | bytes 786432
Async XLA Ops:
  0.0 55.1 %copy-start = (bf16[192,32,2,128]{3,2,1,0:T(2,128)(2,1)S(1)}, bf16[192,32,2,128]{3,2,1,0:T(2,128)(2,1)}, u32[]{:S(2)}) copy-start(bf16[192,32,2,128]{3,2,1,0:T(2,128)(2,1)} %param.18) | copy-start | bytes 9437188
  0.0 55.1 %copy-start.1 = (bf16[2,48,2048]{2,1,0:T(8,128)(2,1)S(1)}, bf16[2,48,2048]{2,1,0:T(8,128)(2,1)}, u32[]{:S(2)}) copy-start(bf16[2,48,2048]{2,1,0:T(8,128)(2,1)} %x_hbm.1) | copy-start | bytes 1179652
  0.0 55.1 %copy-start.2 = (s32[48,4]{0,1:T(4,128)S(1)}, s32[48,4]{0,1:T(4,128)}, u32[]{:S(2)}) copy-start(s32[48,4]{0,1:T(4,128)} %param.22) | copy-start | bytes 2308
  0.0 55.1 %copy-start.3 = (s32[48]{0:T(128)S(1)}, s32[48]{0:T(128)}, u32[]{:S(2)}) copy-start(s32[48]{0:T(128)} %param.23) | copy-start | bytes 580
  0.0 55.1 %copy-start.4 = (s32[48]{0:T(128)S(1)}, s32[48]{0:T(128)}, u32[]{:S(2)}) copy-start(s32[48]{0:T(128)} %param.17) | copy-start | bytes 580

commit v6 on v5

--- a/solution.py
+++ b/solution.py
@@ -402,6 +402,11 @@
     others = got_picks.at[pl.ds(1, POOL - 1)]
     pltpu.make_async_copy(others, others, pick_send).wait()
     pltpu.make_async_copy(parts, parts, part_send).wait()
+
+
+def far_first(i):
+    j = i % BATCH
+    return i - j + (j % C) * Z + (j // C + 3) % Z
 
 
 def shared_chip_kernel(
@@ -575,7 +580,9 @@
     push(down_hbm, down.at[my_part], weight_send.at[0], weight_recv.at[0], other)
     for b in range(1, BATCHES):
         build(b, sent)
-        lax.fori_loop(b * BATCH, (b + 1) * BATCH, send_row, 0)
+        lax.fori_loop(
+            b * BATCH, (b + 1) * BATCH, lambda i, _: send_row(far_first(i), 0), 0
+        )
         if b == 1:
             push(up_hbm, up.at[my_part], weight_send.at[1], weight_recv.at[1], other)
     got[pl.ds(0, three)] = sent[pl.ds(0, three)]
@@ -651,7 +658,11 @@
 
         if b == 0:
             returned[pl.ds(0, three)] = answers[pl.ds(0, three)]
-        lax.fori_loop(max(b * BATCH, 1), (b + 1) * BATCH, answer, 0)
+            lax.fori_loop(1, BATCH, answer, 0)
+        else:
+            lax.fori_loop(
+                b * BATCH, (b + 1) * BATCH, lambda i, _: answer(far_first(i), 0), 0
+            )
 
     loads[2].wait()
     await_bytes(down.at[my_part], weight_recv.at[0])

time: 56.2 us -> 56.4 us (level)
  no operation moved by 1% of the time
where the time goes in v6:
time: 56.4 us
  Pallas kernels  54.7 us (97%)
  local copies, waits for them, and re-layouts  0.77 us (1%)
  between operations  0.69 us (1%)
    pallas_call x1, Pallas kernels, shared_chip(): pl.pallas_call(functools.partial(shared_chip_kernel, rows, ctx, page), ou...  54.7 us

profile of v6, /device:TPU:1, one launch (start us, length us, event | category | flops | bytes accessed | tf_op | source)
XLA Modules:
  0.0 56.4 jit_solution(15100255392168933630)
XLA Ops:
  0.0 0.0 copy-start
  0.0 0.0 copy-start.1
  0.0 0.0 copy-start.2
  0.0 0.0 copy-start.3
  0.0 0.0 copy-start.4
  0.0 54.7 %shared_chip_and_attention.1 = (bf16[2,48,2048]{2,1,0:T(8,128)(2,1)S(1)}, s32[1,1]{1,0:T(1,128)}) custom-call(s32[1,48]{1,0:T(1,128)} %bitcast.32, s32[4,48]{1,0:T(4,128)} %bitcast.28, s32[1,48]{1,0:T(1,128)} %bitcast.30, bf16[2,48,2048]{2,1,0:T(8,128)(2,1)} %x_hbm.1, bf16[2,48,2048]{2,1,0:T(8,128)(2,1)} %base_hbm.1, bf16[512,2048]{1,0:T(8,128)(2,1)} %bitcast.19, ...), custom_call_target="tpu_custom_call" | custom-call | flops 3000000000 | bytes 12000000 | tf_op jit(solution)/shard_map/shared_chip_and_attention/pallas_call | solution.py:778
  55.4 0.0 copy-done
  55.4 0.0 copy-done.1
  55.4 0.0 copy-done.2
  55.4 0.0 copy-done.3
  55.4 0.0 copy-done.4
  55.4 0.2 conditional.1
  55.6 0.7 %copy.17 = bf16[2,48,2048]{2,1,0:T(8,128)(2,1)} copy(bf16[2,48,2048]{2,1,0:T(8,128)(2,1)S(1)} %get-tuple-element.49) | data formatting | bytes 786432
Async XLA Ops:
  0.0 55.4 %copy-start = (bf16[192,32,2,128]{3,2,1,0:T(2,128)(2,1)S(1)}, bf16[192,32,2,128]{3,2,1,0:T(2,128)(2,1)}, u32[]{:S(2)}) copy-start(bf16[192,32,2,128]{3,2,1,0:T(2,128)(2,1)} %param.18) | copy-start | bytes 9437188
  0.0 55.4 %copy-start.1 = (bf16[2,48,2048]{2,1,0:T(8,128)(2,1)S(1)}, bf16[2,48,2048]{2,1,0:T(8,128)(2,1)}, u32[]{:S(2)}) copy-start(bf16[2,48,2048]{2,1,0:T(8,128)(2,1)} %x_hbm.1) | copy-start | bytes 1179652
  0.0 55.4 %copy-start.2 = (s32[48,4]{0,1:T(4,128)S(1)}, s32[48,4]{0,1:T(4,128)}, u32[]{:S(2)}) copy-start(s32[48,4]{0,1:T(4,128)} %param.22) | copy-start | bytes 2308
  0.0 55.4 %copy-start.3 = (s32[48]{0:T(128)S(1)}, s32[48]{0:T(128)}, u32[]{:S(2)}) copy-start(s32[48]{0:T(128)} %param.23) | copy-start | bytes 580
  0.0 55.4 %copy-start.4 = (s32[48]{0:T(128)S(1)}, s32[48]{0:T(128)}, u32[]{:S(2)}) copy-start(s32[48]{0:T(128)} %param.17) | copy-start | bytes 580
